TPU v7x, 256 devices: a whole 4x4x8 slice. The times are simulated.
256 devices in a mesh: row: 16 (over y, x), col: 8 (over z), feat: 2 (over core).
Axes of the slice: x: 4, y: 4, z: 8, core: 2. Of those that a mesh axis runs over, the one named last changes fastest.
Arguments:
- tiles: bfloat16 [16, 8, 128, 128, 128], P('row', 'col'), may hold values from -0.0625 to 0.0625
- coords: int32 [16, 8, 128, 2], P('row', 'col'), may hold values from 0 to 15, as said below
- counts: int32 [16, 8], P('row', 'col'), may hold values from 16 to 128, as said below
- features: bfloat16 [16384, 1024], P(('col', 'row')), may hold values from -24 to 24
- weight: bfloat16 [1024, 1024], P(None, 'feat'), may hold values from -0.1875 to 0.1875
- grad_out: bfloat16 [32768, 1024], P('row', 'feat'), may hold values from -6 to 6
Outputs:
- layer_out: bfloat16 [32768, 1024], P('row', 'feat')
- weight_grad: float32 [1024, 1024], P(('row', 'col'), 'feat')
- input_grad: bfloat16 [16384, 1024], P(('col', 'row'), 'feat')
Inputs may be any that keep to these rules, and one draw needn't show every extreme that they name: `coords`: column 0 is a tile row below 16, column 1 a tile column below 16; the slots of one block name distinct tiles. Slots 0 to counts - 1 of a block are live, the others are to be ignored.
All inputs are finite; a program needn't handle non-finite values.
Results may differ from a plain program's by a relative error of at most 0.017.
Values may be sent and summed in bfloat16 or wider, within the bound.
A program may use at most 128 MiB of HBM per device.

v0:
```python
import math

import jax
import jax.numpy as jnp
from jax import lax
from jax.sharding import PartitionSpec as P


def silu_slope(value):
    sig = jax.nn.sigmoid(value)
    return sig * (1.0 + value * (1.0 - sig))


def tile_product(tiles, coords, count, dense, out_tiles, backward):
    slots, edge = (tiles.shape[0], tiles.shape[1])
    width = dense.shape[1]
    dense_tiles = dense.reshape(-1, edge, width)
    step = math.gcd(slots, 32)
    targets = jnp.arange(out_tiles, dtype=jnp.int32)
    source_col = 0 if backward else 1
    target_col = 1 if backward else 0
    form = "kji,kjh->kih" if backward else "kij,kjh->kih"

    def advance(index, total):
        first = index * step
        block_tiles = lax.dynamic_slice_in_dim(tiles, first, step, 0)
        block_coords = lax.dynamic_slice_in_dim(coords, first, step, 0)
        live = (first + jnp.arange(step, dtype=jnp.int32) < count).astype(jnp.float32)
        picked = dense_tiles[block_coords[:, source_col]]
        prod = jnp.einsum(form, block_tiles, picked, preferred_element_type=jnp.float32)
        onehot = (block_coords[:, target_col][None, :] == targets[:, None]).astype(
            jnp.float32
        ) * live[None, :]
        return total + jnp.einsum("rk,kih->rih", onehot, prod)

    start = jnp.zeros((out_tiles, edge, width), jnp.float32)
    total = lax.fori_loop(0, slots // step, advance, start)
    return total.reshape(out_tiles * edge, width)


def on_device(tiles, coords, counts, features, weight, grad_out):
    block_tiles = tiles[0, 0]
    block_coords = coords[0, 0]
    block_count = counts[0, 0]
    edge = block_tiles.shape[1]
    row_count = grad_out.shape[0] // edge
    projected = jnp.dot(features, weight, preferred_element_type=jnp.float32).astype(jnp.bfloat16)
    column_block = lax.all_gather(projected, "row", axis=0, tiled=True)
    col_count = column_block.shape[0] // edge
    partial_value = tile_product(
        block_tiles, block_coords, block_count, column_block, row_count, False
    )
    pre = lax.psum(partial_value, "col")
    layer_out = jax.nn.silu(pre).astype(jnp.bfloat16)
    delta = (grad_out.astype(jnp.float32) * silu_slope(pre)).astype(jnp.bfloat16)
    back_partial = tile_product(block_tiles, block_coords, block_count, delta, col_count, True)
    back = lax.psum_scatter(back_partial, "row", scatter_dimension=0, tiled=True).astype(
        jnp.bfloat16
    )
    node_total = features.shape[0] * lax.axis_size("row") * lax.axis_size("col")
    scale = node_total ** (-0.5)
    product = lax.dot_general(
        features, back, (((0,), (0,)), ((), ())), preferred_element_type=jnp.float32
    )
    weight_grad = lax.psum_scatter(product * scale, ("row", "col"), scatter_dimension=0, tiled=True)
    input_terms = lax.dot_general(
        back, weight, (((1,), (1,)), ((), ())), preferred_element_type=jnp.float32
    )
    input_grad = lax.psum_scatter(input_terms, "feat", scatter_dimension=1, tiled=True).astype(
        jnp.bfloat16
    )
    return (layer_out, weight_grad, input_grad)


def solution(mesh):
    return jax.shard_map(
        on_device,
        mesh=mesh,
        in_specs=(
            P("row", "col", None, None, None),
            P("row", "col", None, None),
            P("row", "col"),
            P(("col", "row"), None),
            P(None, "feat"),
            P("row", "feat"),
        ),
        out_specs=(P("row", "feat"), P(("row", "col"), "feat"), P(("col", "row"), "feat")),
        check_vma=False,
    )
```

profile of v0, /device:TPU:2, one launch (start us, length us, event | category | flops | bytes accessed | tf_op | source)
XLA Modules:
  0.0 1125.8 jit_solution(5435252110262531265)
XLA Ops:
  10.4 53.2 %all-gather.2.cloned.1.call-done = bf16[2048,512]{1,0:T(8,128)(2,1)} async-done(((bf16[128,512]{1,0:T(8,128)(2,1)}), bf16[2048,512]{1,0:T(8,128)(2,1)}) %all-gather.2.cloned.1.call-update) | async-done | bytes 2097168 | tf_op jit(solution)/shard_map/all_gather | solution.py:48
  63.6 79.0 %while.28 = (s32[]{:T(128)}, f32[16,128,512]{2,0,1:T(8,128)}, s32[128,2]{0,1:T(2,128)}, s32[]{:T(128)}, bf16[128,128,128]{2,1,0:T(8,128)(2,1)}, /*index=5*/bf16[...) while((s32[]{:T(128)}, f32[16,128,512]{2,0,1:T(8,128)}, ...), condition=%wide.region_1.0_spmd.clone, body=%wide.region_0.0_spmd.clone.sunk | while | flops 606079232 | bytes 30414508 | solution.py:37
  64.4 4.4 gather_fusion
  68.8 5.7 fusion.55
  75.1 7.3 select_add_fusion.4
  83.2 4.4 gather_fusion
  87.5 5.7 fusion.55
  93.9 8.6 select_add_fusion.4
  103.2 4.4 gather_fusion
  107.6 5.7 fusion.55
  114.0 8.6 select_add_fusion.4
  123.3 4.4 gather_fusion
  127.7 5.7 fusion.55
  134.0 8.6 select_add_fusion.4
  142.6 6.6 copy.18
  149.4 6.4 copy.16
  155.8 102.3 %all-reduce.2.cloned.1.call-done = f32[2048,512]{1,0:T(8,128)} async-done(((f32[2048,512]{1,0:T(8,128)}), f32[2048,512]{1,0:T(8,128)}) %all-reduce.2.cloned.1.call-update) | async-done | bytes 4194320 | tf_op jit(solution)/shard_map/psum | solution.py:53
  258.1 4.7 multiply_convert_fusion
  262.7 69.7 %while.29 = (s32[]{:T(128)}, f32[16,128,512]{2,0,1:T(8,128)}, s32[128,2]{0,1:T(2,128)S(1)}, s32[]{:T(128)}, bf16[128,128,128]{1,2,0:T(8,128)(2,1)}, /*index=5*/b...) while((s32[]{:T(128)}, f32[16,128,512]{2,0,1:T(8,128)}, ...), condition=%wide.region_4.5_spmd.clone, body=%wide.region_3.4_spmd.clone.sunk | while | flops 606079232 | bytes 30414508 | solution.py:37
  262.8 2.8 gather_fusion.1
  265.6 5.7 fusion.60
  272.0 7.2 select_add_fusion.5
  282.1 5.7 fusion.60
  288.5 8.5 select_add_fusion.5
  299.8 5.7 fusion.60
  306.2 8.5 select_add_fusion.5
  317.6 5.7 fusion.60
  324.0 8.5 select_add_fusion.5
  332.5 6.6 copy.19
  339.1 81.2 %reduce-scatter.6.cloned.1.call-done = f32[128,512]{1,0:T(8,128)} async-done(((f32[2048,512]{1,0:T(8,128)}), f32[128,512]{1,0:T(8,128)}) %reduce-scatter.6.cloned.1.call-update) | async-done | bytes 262160 | tf_op jit(solution)/shard_map/reduce_scatter | solution.py:57
  425.9 10.0 reduce-scatter.8.cloned.1.call-done
  437.5 681.8 %reduce-scatter.10.cloned.1.call-done = f32[8,512]{1,0:T(8,128)} async-done(((f32[1024,512]{1,0:T(8,128)}), f32[8,512]{1,0:T(8,128)}) %reduce-scatter.10.cloned.1.call-update) | async-done | bytes 16400
  (58 shorter events, 27.6 us)
Async XLA Ops:
  7.2 1.2 copy-start
  7.2 56.5 %all-gather.2.cloned.1.call-start = ((), (), s32[]{:S(2)}) async-start(), calls=%async_computation.3 | async-start | bytes 2228224 | tf_op jit(solution)/shard_map/all_gather | solution.py:48
  10.3 247.7 %all-reduce.2.cloned.1.call-start = ((), (), s32[]{:S(2)}) async-start(), calls=%async_computation.4 | async-start | bytes 8388608 | tf_op jit(solution)/shard_map/psum | solution.py:53
  149.2 271.2 %reduce-scatter.6.cloned.1.call-start = ((), (), s32[]{:S(2)}) async-start(), calls=%async_computation.5 | async-start | bytes 4456448 | tf_op jit(solution)/shard_map/reduce_scatter | solution.py:57
  155.8 106.9 %copy-start.2 = (s32[128,2]{0,1:T(2,128)S(1)}, s32[128,2]{0,1:T(2,128)}, u32[]{:S(2)}) copy-start(s32[128,2]{0,1:T(2,128)} %get-tuple-element.506) | copy-start | bytes 3076
  339.1 83.6 %copy-start.1 = (bf16[128,1024]{1,0:T(8,128)(2,1)S(1)}, bf16[128,1024]{1,0:T(8,128)(2,1)}, u32[]{:S(2)}) copy-start(bf16[128,1024]{1,0:T(8,128)(2,1)} %param.13) | copy-start | bytes 786436
  339.1 96.8 %reduce-scatter.8.cloned.1.call-start = ((), (), s32[]{:S(2)}) async-start(), calls=%async_computation.6 | async-start | bytes 786432 | tf_op jit(solution)/shard_map/reduce_scatter | solution.py:69
  422.6 696.7 %reduce-scatter.10.cloned.1.call-start = ((), (), s32[]{:S(2)}) async-start(), calls=%async_computation.7 | async-start | bytes 2113536
Sparse Core Ops, SparseCore 0:
  11.0 52.5 all-gather.1
  149.3 108.7 all-reduce.1
  339.2 81.1 reduce-scatter.5
  422.9 12.9 reduce-scatter.7
  438.8 680.4 reduce-scatter.9
where the time goes:
time: 1150 us; the launch traced here: 1130 us
  waiting for transfers between devices  929 us (81%)
  matrix products  117 us (10%)
  local copies, waits for them, and re-layouts  54.4 us (5%)
  between operations  13.8 us (1%)
  other arithmetic  11.6 us (1%)
    unnamed x6, waiting for transfers between devices  682 us
    psum x1, waiting for transfers between devices, on_device(): pre = lax.psum(partial_value, 'col')  102 us
    reduce_scatter x1, waiting for transfers between devices, on_device(): lax.psum_scatter(back_partial, 'row', scatter_dimension=0, tiled=True)  81.2 us
    dot_general x8, matrix products, advance(): return total + jnp.einsum('rk,kih->rih', onehot, prod)  65.7 us
    all_gather x1, waiting for transfers between devices, on_device(): column_block = lax.all_gather(projected, 'row', axis=0, tiled=True)  53.2 us
    dot_general x8, matrix products, advance(): jnp.einsum(form, block_tiles, picked, preferred_element_type=jnp.float32)  45.7 us
    gather x8, local copies, waits for them, and re-layouts, advance(): picked = dense_tiles[block_coords[:, source_col]]  28.6 us
  transfers between devices with their start and end apart: 5, of which 5 were waited for; matrix products, arithmetic and copies ran while one was open for 1% of the time, Pallas kernels for 0%

commit v1 on v0

v1 whole, which is shorter than its diff:
```python
import jax
import jax.numpy as jnp
from jax import lax
from jax.sharding import PartitionSpec as P

BF16 = jnp.bfloat16
F32 = jnp.float32


def silu_slope(value):
    sig = jax.nn.sigmoid(value)
    return sig * (1.0 + value * (1.0 - sig))


def densify(tiles, coords, count, row_tiles, col_tiles):
    slots, edge = tiles.shape[0], tiles.shape[1]
    place = coords[:, 0] * col_tiles + coords[:, 1]
    slot = jnp.arange(slots, dtype=jnp.int32)
    cell = jnp.arange(row_tiles * col_tiles, dtype=jnp.int32)
    hit = (place[None, :] == cell[:, None]) & (slot[None, :] < count)
    where_from = jnp.sum(jnp.where(hit, slot[None, :], 0), axis=1)
    live = jnp.any(hit, axis=1)
    picked = jnp.where(live[:, None, None], tiles[where_from], jnp.zeros((), tiles.dtype))
    dense = picked.reshape(row_tiles, col_tiles, edge, edge).transpose(0, 2, 1, 3)
    return dense.reshape(row_tiles * edge, col_tiles * edge)


def on_device(tiles, coords, counts, features, weight, grad_out):
    edge = tiles.shape[-1]
    row_tiles = grad_out.shape[0] // edge
    col_tiles = features.shape[0] * lax.axis_size("row") // edge
    dense = densify(tiles[0, 0], coords[0, 0], counts[0, 0], row_tiles, col_tiles)
    projected = jnp.dot(features, weight, preferred_element_type=F32).astype(BF16)
    column_block = lax.all_gather(projected, "row", axis=0, tiled=True)
    partial_value = jnp.dot(dense, column_block, preferred_element_type=F32).astype(BF16)
    own = lax.psum_scatter(partial_value, "col", scatter_dimension=0, tiled=True)
    pre = lax.all_gather(own, "col", axis=0, tiled=True).astype(F32)
    layer_out = jax.nn.silu(pre).astype(BF16)
    delta = (grad_out.astype(F32) * silu_slope(pre)).astype(BF16)
    back_partial = lax.dot_general(
        dense, delta, (((0,), (0,)), ((), ())), preferred_element_type=F32
    ).astype(BF16)
    back = lax.psum_scatter(back_partial, "row", scatter_dimension=0, tiled=True)
    node_total = features.shape[0] * lax.axis_size("row") * lax.axis_size("col")
    scale = node_total ** (-0.5)
    product = lax.dot_general(
        features, back, (((0,), (0,)), ((), ())), preferred_element_type=F32
    )
    summed = lax.psum_scatter((product * scale).astype(BF16), "row", scatter_dimension=0, tiled=True)
    weight_grad = lax.psum_scatter(summed, "col", scatter_dimension=0, tiled=True).astype(F32)
    input_terms = lax.dot_general(
        back, weight, (((1,), (1,)), ((), ())), preferred_element_type=F32
    ).astype(BF16)
    input_grad = lax.psum_scatter(input_terms, "feat", scatter_dimension=1, tiled=True)
    return (layer_out, weight_grad, input_grad)


def solution(mesh):
    return jax.shard_map(
        on_device,
        mesh=mesh,
        in_specs=(
            P("row", "col", None, None, None),
            P("row", "col", None, None),
            P("row", "col"),
            P(("col", "row"), None),
            P(None, "feat"),
            P("row", "feat"),
        ),
        out_specs=(P("row", "feat"), P(("row", "col"), "feat"), P(("col", "row"), "feat")),
        check_vma=False,
    )
```

time: 1150 us -> 390 us (0.34); the launches traced: 1130 us -> 388 us
  waiting for transfers between devices: 929 us -> 318 us
  matrix products: 117 us -> 25.6 us
  local copies, waits for them, and re-layouts: 54.4 us -> 14.7 us
    unnamed x6 -> x9, waiting for transfers between devices: 682 us -> 114 us
    psum x1 -> x0, waiting for transfers between devices: 102 us -> none  [on_device(): pre = lax.psum(partial_value, 'col')]
    dot_general x17 -> x3, matrix products: 113 us -> 23 us  [the longest x1 11.3 us: on_device(): lax.dot_general(dense, delta, (((0,), (0,)), ((), ())), preferred_element...]
    reduce_scatter x0 -> x1, waiting for transfers between devices: none -> 41.8 us  [on_device(): lax.psum_scatter(partial_value, 'col', scatter_dimension=0, tiled=True)]
    all_gather x0 -> x1, waiting for transfers between devices: none -> 41.7 us  [on_device(): pre = lax.all_gather(own, 'col', axis=0, tiled=True).astype(F32)]
    all_gather x1, waiting for transfers between devices: 53.2 us -> 29.5 us  [on_device(): column_block = lax.all_gather(projected, 'row', axis=0, tiled=True)]
    gather x8 -> x1, local copies, waits for them, and re-layouts: 28.6 us -> 10.5 us  [densify(): tiles[where_from]]
    while x2 -> x0, local copies, waits for them, and re-layouts: 13.2 us -> none  [tile_product(): total = lax.fori_loop(0, slots // step, advance, start)]
  transfers between devices with their start and end apart: 5 -> 7, of which waited for: 5 -> 7; matrix products, arithmetic and copies ran while one was open for 1% -> 7% of each run, Pallas kernels for 0% -> 0%
where the time goes in v1:
time: 390 us; the launch traced here: 388 us
  waiting for transfers between devices  318 us (82%)
  matrix products  25.6 us (7%)
  other arithmetic  15 us (4%)
  between operations  14.8 us (4%)
  local copies, waits for them, and re-layouts  14.7 us (4%)
    unnamed x9, waiting for transfers between devices  114 us
    reduce_scatter x1, waiting for transfers between devices, on_device(): lax.psum_scatter(back_partial, 'row', scatter_dimension=0, tiled=True)  77.6 us
    reduce_scatter x1, waiting for transfers between devices, on_device(): lax.psum_scatter(partial_value, 'col', scatter_dimension=0, tiled=True)  41.8 us
    all_gather x1, waiting for transfers between devices, on_device(): pre = lax.all_gather(own, 'col', axis=0, tiled=True).astype(F32)  41.7 us
    all_gather x1, waiting for transfers between devices, on_device(): column_block = lax.all_gather(projected, 'row', axis=0, tiled=True)  29.5 us
    reduce_scatter x1, waiting for transfers between devices, on_device(): lax.psum_scatter(input_terms, 'feat', scatter_dimension=1, tiled=True)  13.2 us
    select_n x1, other arithmetic, densify(): jnp.where(live[:, None, None], tiles[where_from], jnp.zeros((), tiles.dty...  11.5 us
    dot_general x1, matrix products, on_device(): lax.dot_general(dense, delta, (((0,), (0,)), ((), ())), preferred_element...  11.3 us
  transfers between devices with their start and end apart: 7, of which 7 were waited for; matrix products, arithmetic and copies ran while one was open for 7% of the time, Pallas kernels for 0%

profile of v1, /device:TPU:2, one launch (start us, length us, event | category | flops | bytes accessed | tf_op | source)
XLA Modules:
  0.0 388.2 jit_solution(13215583671676130153)
XLA Ops:
  7.2 0.0 all-gather.3.cloned.1.call-start
  7.2 1.2 copy-done
  8.4 1.9 convolution_convert_fusion.1
  10.3 0.0 all-gather.3.cloned.1.call-update
  10.3 0.0 reduce-scatter.10.cloned.1.call-start
  11.0 0.8 add_bitcast_fusion
  11.8 0.1 fusion.24
  11.9 0.1 broadcast_in_dim.32
  12.0 0.1 select_reduce_fusion
  12.2 10.5 %gather_fusion = bf16[256,128,128]{2,1,0:T(8,128)(2,1)} fusion(bf16[128,128,128]{2,1,0:T(8,128)(2,1)} %bitcast.33, s32[1024]{0:T(1024)S(1)} %pad_clamp_fusion), kind=kCustom, calls=%fused_computation | custom fusion | bytes 16778240 | tf_op jit(solution)/shard_map/gather | solution.py:23
  22.7 11.5 %copy_select_fusion = bf16[16,16,128,128]{3,1,2,0:T(8,128)(2,1)} fusion(bf16[16,16,128,128]{3,2,1,0:T(8,128)(2,1)} %bitcast.32, pred[16,16]{1,0:T(8,128)(4,1)S(1)} %broadcast_in_dim.32), kind=kLoop, calls=%fused_computation.5 | loop fusion | flops 4194304 | bytes 16777472 | tf_op jit(solution)/shard_map/jit(_where)/select_n | solution.py:23
  34.1 29.5 %all-gather.3.cloned.1.call-done = bf16[2048,512]{1,0:T(8,128)(2,1)} async-done(((bf16[128,512]{1,0:T(8,128)(2,1)}), bf16[2048,512]{1,0:T(8,128)(2,1)}) %all-gather.3.cloned.1.call-update) | async-done | bytes 2097168 | tf_op jit(solution)/shard_map/all_gather | solution.py:34
  63.6 9.8 %fusion.17 = bf16[2048,512]{1,0:T(8,128)(2,1)} fusion(bf16[2048,512]{1,0:T(8,128)(2,1)} %all-gather.3.cloned.1.call-done, bf16[256,8,16,128]{3,2,1,0:T(8,128)(2,1)} %bitcast.34), kind=kOutput, calls=%fused_computation.20 | convolution fusion | flops 4296015872 | bytes 12582912 | tf_op jit(solution)/shard_map/dot_general | solution.py:35
  73.5 0.0 reduce-scatter.10.cloned.1.call-update
  73.5 0.0 all-gather.5.cloned.1.call-start
  73.5 41.8 %reduce-scatter.10.cloned.1.call-done = bf16[256,512]{1,0:T(8,128)(2,1)} async-done(((bf16[2048,512]{1,0:T(8,128)(2,1)}), bf16[256,512]{1,0:T(8,128)(2,1)}) %reduce-scatter.10.cloned.1.call-update) | async-done | bytes 262160 | tf_op jit(solution)/shard_map/reduce_scatter | solution.py:36
  115.4 0.2 reduce-scatter.12.cloned.1.call-start
  115.6 41.7 %all-gather.5.cloned.1.call-done = bf16[2048,512]{1,0:T(8,128)(2,1)} async-done(((bf16[256,512]{1,0:T(8,128)(2,1)}), bf16[2048,512]{1,0:T(8,128)(2,1)}) %all-gather.5.cloned.1.call-update) | async-done | bytes 2097168 | tf_op jit(solution)/shard_map/all_gather | solution.py:37
  157.3 11.3 %fusion.14 = bf16[2048,512]{1,0:T(8,128)(2,1)} fusion(bf16[256,8,16,128]{3,2,1,0:T(8,128)(2,1)} %bitcast.35, bf16[2048,512]{1,0:T(8,128)(2,1)} %all-gather.5.cloned.1.call-done, bf16[2048,512]{1,0:T(8,128)(2,1)} %param.11), kind=kOutput, calls=%fused_computation.19 | convolution fusion | flops 4307550208 | bytes 14680064 | tf_op jit(solution)/shard_map/dot_general | solution.py:40
  168.6 0.0 reduce-scatter.16.cloned.1.call-start
  168.7 77.6 %reduce-scatter.12.cloned.1.call-done = bf16[128,512]{1,0:T(8,128)(2,1)} async-done(((bf16[2048,512]{1,0:T(8,128)(2,1)}), bf16[128,512]{1,0:T(8,128)(2,1)}) %reduce-scatter.12.cloned.1.call-update) | async-done | bytes 131088 | tf_op jit(solution)/shard_map/reduce_scatter | solution.py:43
  246.3 1.4 fusion.22
  247.7 1.3 copy.16
  249.1 0.0 reduce-scatter.18.cloned.1.call-start
  249.1 78.9 %reduce-scatter.16.cloned.1.call-done = bf16[64,512]{1,0:T(8,128)(2,1)} async-done(((bf16[1024,512]{1,0:T(8,128)(2,1)}), bf16[64,512]{1,0:T(8,128)(2,1)}) %reduce-scatter.16.cloned.1.call-update) | async-done | bytes 65552
  328.0 0.0 reduce-scatter.14.cloned.1.call-start
  328.1 1.2 convolution_convert_fusion
  329.3 2.5 fusion.9
  331.8 34.8 %reduce-scatter.18.cloned.1.call-done = bf16[8,512]{1,0:T(8,128)(2,1)} async-done(((bf16[64,512]{1,0:T(8,128)(2,1)}), bf16[8,512]{1,0:T(8,128)(2,1)}) %reduce-scatter.18.cloned.1.call-update) | async-done | bytes 8208
  366.6 0.9 copy.19
  367.4 0.7 copy.15
  368.1 13.2 %reduce-scatter.14.cloned.1.call-done = bf16[128,512]{1,0:T(8,128)(2,1)} async-done(((bf16[128,1024]{1,0:T(8,128)(2,1)}), bf16[128,512]{1,0:T(8,128)(2,1)}) %reduce-scatter.14.cloned.1.call-update) | async-done | bytes 131088 | tf_op jit(solution)/shard_map/reduce_scatter | solution.py:54
  (15 shorter events, 0.1 us)
Async XLA Ops:
  7.2 1.2 copy-start
  7.2 56.5 %all-gather.3.cloned.1.call-start = ((), (), s32[]{:S(2)}) async-start(), calls=%async_computation.5 | async-start | bytes 2228224 | tf_op jit(solution)/shard_map/all_gather | solution.py:34
  10.3 105.0 %reduce-scatter.10.cloned.1.call-start = ((), (), s32[]{:S(2)}) async-start(), calls=%async_computation.6 | async-start | bytes 2359296 | tf_op jit(solution)/shard_map/reduce_scatter | solution.py:36
  73.5 83.9 %all-gather.5.cloned.1.call-start = ((), (), s32[]{:S(2)}) async-start(), calls=%async_computation.7 | async-start | bytes 2359296 | tf_op jit(solution)/shard_map/all_gather | solution.py:37
  115.4 130.9 %copy-start.2 = (bf16[128,1024]{1,0:T(8,128)(2,1)S(1)}, bf16[128,1024]{1,0:T(8,128)(2,1)}, u32[]{:S(2)}) copy-start(bf16[128,1024]{1,0:T(8,128)(2,1)} %param.9) | copy-start | bytes 786436
  115.4 130.9 %reduce-scatter.12.cloned.1.call-start = ((), (), s32[]{:S(2)}) async-start(), calls=%async_computation.8 | async-start | bytes 2228224 | tf_op jit(solution)/shard_map/reduce_scatter | solution.py:43
  168.6 159.4 %reduce-scatter.16.cloned.1.call-start = ((), (), s32[]{:S(2)}) async-start(), calls=%async_computation.10 | async-start | bytes 1114112
  246.3 81.8 %copy-start.3 = (bf16[128,512]{1,0:T(8,128)(2,1)S(1)}, bf16[128,512]{1,0:T(8,128)(2,1)}, u32[]{:S(2)}) copy-start(bf16[128,512]{1,0:T(8,128)(2,1)} %reduce-scatter.12.cloned.1.call-done) | copy-start | bytes 393220
  249.1 80.2 %copy-start.1 = (bf16[2048,512]{1,0:T(8,128)(2,1)S(1)}, bf16[2048,512]{1,0:T(8,128)(2,1)}, u32[]{:S(2)}) copy-start(bf16[2048,512]{1,0:T(8,128)(2,1)} %all-gather.5.cloned.1.call-done) | copy-start | bytes 6291460
  249.1 117.5 %reduce-scatter.18.cloned.1.call-start = ((), (), s32[]{:S(2)}) async-start(), calls=%async_computation.11 | async-start | bytes 73728
  328.0 53.3 %reduce-scatter.14.cloned.1.call-start = ((), (), s32[]{:S(2)}) async-start(), calls=%async_computation.9 | async-start | bytes 393216 | tf_op jit(solution)/shard_map/reduce_scatter | solution.py:54
Sparse Core Ops, SparseCore 0:
  11.0 52.5 all-gather.2
  73.6 41.7 reduce-scatter.9
  117.2 40.1 all-gather.4
  168.8 77.4 reduce-scatter.11
  250.6 77.3 reduce-scatter.15
  330.4 36.1 reduce-scatter.17
  369.8 11.5 reduce-scatter.13

commit v2 on v1

v2 whole, which is shorter than its diff:
```python
import functools

import jax
import jax.numpy as jnp
from jax import lax
from jax.experimental import pallas as pl
from jax.experimental.pallas import tpu as pltpu
from jax.sharding import PartitionSpec as P

BF16 = jnp.bfloat16
F32 = jnp.float32
MESH = pl.DeviceIdType.MESH
VMEM = pltpu.VMEM

SIDE = 4
DEPTH = 8
TILE = 128
ROWS = 2048
SLAB = ROWS // DEPTH
HALF = SLAB // 2
WIDE = 512
INNER = 1024
CHUNKS = 2
HC = WIDE // CHUNKS
STAGGER = 2

DN_T = (((0,), (0,)), ((), ()))
DN_N = (((1,), (1,)), ((), ()))


def f32dot(a, b, dims=(((1,), (0,)), ((), ()))):
    return lax.dot_general(a, b, dims, preferred_element_type=F32)


def kernel(
    slot_of, tiles_hbm, feat_hbm, weight_hbm, gout_hbm,
    layer_hbm, wgrad, igrad,
    tiles, adj, feat, weight, gout, layer,
    gath, part, zsend_p, zsend_m, zrecv_p, zrecv_m, pre, delta, bpart, back,
    wpart, wown, wz, terms, terms_send, terms_recv,
    bs1, bs2, bs3, bs4, br1, br2, br3, br4, bown,
    ws1, ws2, ws3, ws4, wr1, wr2, wr3, wr4, wsum,
    local_sem, out_sem, send_sem, recv_sem,
):
    row = lax.axis_index("row")
    z = lax.axis_index("col")
    f = lax.axis_index("feat")
    y, x = row // SIDE, row % SIDE

    def at(dy, dx, dz):
        return (((y + dy + SIDE) % SIDE) * SIDE + (x + dx + SIDE) % SIDE, (z + dz + DEPTH) % DEPTH, f)

    xp, xm = at(0, 1, 0), at(0, -1, 0)
    yp, ym = at(1, 0, 0), at(-1, 0, 0)
    zpeer = [None] + [at(0, 0, d) for d in range(1, DEPTH)]
    zp, zm = zpeer[1], zpeer[DEPTH - 1]
    other = (row, z, 1 - f)

    loads = [
        pltpu.make_async_copy(weight_hbm, weight, local_sem.at[0]),
        pltpu.make_async_copy(feat_hbm, feat, local_sem.at[1]),
        pltpu.make_async_copy(tiles_hbm, tiles.at[0:TILE], local_sem.at[2]),
        pltpu.make_async_copy(gout_hbm, gout, local_sem.at[3]),
    ]
    for load in loads:
        load.start()

    barrier = pltpu.get_barrier_semaphore()
    partners = [xp, xm, yp, ym, other] + zpeer[1:]
    for device in partners:
        pl.semaphore_signal(barrier, inc=1, device_id=device, device_id_type=MESH)

    sent = []

    def send(src, dst, to):
        n = len(sent)
        copy = pltpu.make_async_remote_copy(
            src_ref=src, dst_ref=dst, send_sem=send_sem.at[n], recv_sem=recv_sem.at[n],
            device_id=to, device_id_type=MESH,
        )
        copy.start()
        sent.append(copy)
        return copy

    def arrive(copies):
        for copy in copies:
            copy.wait_recv()

    def lay_out(first, count):
        def one(n, carry):
            slab = first + n // 2
            tile_row = ((z + slab) % DEPTH) * 2 + n % 2
            start = pl.multiple_of((slab * 2 + n % 2) * TILE, TILE)
            for i in range(SIDE):
                for j in range(SIDE):
                    tile_col = ((y + i) % SIDE) * SIDE + (x + j) % SIDE
                    slot = slot_of[tile_row * SIDE * SIDE + tile_col]
                    c = (i * SIDE + j) * TILE
                    adj[pl.ds(start, TILE), c : c + TILE] = tiles[slot]
            return carry

        lax.fori_loop(0, 2 * count, one, 0)

    def scatter_sum(first, last, acc, s1, s2, s3, s4, r1, r2, r3, r4, own, q):
        for t in range(SIDE):
            s1[0, t] = acc(2, t, 0, q).astype(BF16)
            s1[1, t] = acc(2, t, q, 2 * q).astype(BF16)
        c1 = [send(s1.at[d], r1.at[d], first[d]) for d in range(2)]
        yield
        arrive(c1)
        for t in range(SIDE):
            s2[0, t, 0:q] = (acc(1, t, 0, q) + r1[0, t].astype(F32)).astype(BF16)
            s2[0, t, q : 2 * q] = acc(1, t, q, 2 * q).astype(BF16)
            s2[1, t, 0:q] = acc(3, t, 0, q).astype(BF16)
            s2[1, t, q : 2 * q] = (acc(3, t, q, 2 * q) + r1[1, t].astype(F32)).astype(BF16)
        c2 = [send(s2.at[d], r2.at[d], first[d]) for d in range(2)]
        yield
        arrive(c2)
        for t in (2, 1, 3, 0):
            own[t] = acc(0, t, 0, 2 * q) + r2[0, t].astype(F32) + r2[1, t].astype(F32)
            if t == 2:
                s3[0] = own[2, 0:q].astype(BF16)
                s3[1] = own[2, q : 2 * q].astype(BF16)
                c3 = [send(s3.at[d], r3.at[d], last[d]) for d in range(2)]
        yield
        arrive(c3)
        s4[0, 0:q] = (own[1, 0:q] + r3[0].astype(F32)).astype(BF16)
        s4[0, q : 2 * q] = own[1, q : 2 * q].astype(BF16)
        s4[1, 0:q] = own[3, 0:q].astype(BF16)
        s4[1, q : 2 * q] = (own[3, q : 2 * q] + r3[1].astype(F32)).astype(BF16)
        c4 = [send(s4.at[d], r4.at[d], last[d]) for d in range(2)]
        yield
        arrive(c4)
        return own[0] + r4[0].astype(F32) + r4[1].astype(F32)

    def together(flows):
        results = [None] * len(flows)
        live = list(range(len(flows)))
        while live:
            for n in list(live):
                try:
                    next(flows[n])
                except StopIteration as stop:
                    results[n] = stop.value
                    live.remove(n)
            if live:
                yield
        return results

    def activate(k, i):
        start = pl.multiple_of(((z + i) % DEPTH) * SLAB, SLAB)
        cols = slice(k * HC, (k + 1) * HC)
        value = pre[k, i].astype(F32)
        sig = 1.0 / (1.0 + jnp.exp(-value))
        layer[pl.ds(start, SLAB), cols] = (value * sig).astype(BF16)
        slope = sig * (1.0 + value * (1.0 - sig))
        delta[k, i * SLAB : (i + 1) * SLAB] = (gout[pl.ds(start, SLAB), cols].astype(F32) * slope).astype(BF16)

    def flow(k):
        cols = slice(k * HC, (k + 1) * HC)
        if k == 0:
            loads[0].wait()
            loads[1].wait()
            for n in range(CHUNKS):
                gath[n, 0, 0] = f32dot(feat[...], weight[:, n * HC : (n + 1) * HC]).astype(BF16)
            pl.semaphore_wait(barrier, len(partners))
        g = gath.at[k]
        h, q = TILE // 2, TILE // 4
        c = [
            send(g.at[0, 0, 0:h], g.at[0, 3, 0:h], xp),
            send(g.at[0, 0, 0:h], g.at[0, 1, 0:h], xm),
            send(g.at[0, 0, h:TILE], g.at[3, 0, h:TILE], yp),
            send(g.at[0, 0, h:TILE], g.at[1, 0, h:TILE], ym),
        ]
        if k == 0:
            loads[2].wait()
            tiles[TILE] = jnp.zeros((TILE, TILE), BF16)
            lay_out(3, 3)
        yield
        arrive(c)
        c = [
            send(g.at[0, 3, 0:q], g.at[0, 2, 0:q], xp),
            send(g.at[0, 1, q:h], g.at[0, 2, q:h], xm),
            send(g.at[3, 0, h : h + q], g.at[2, 0, h : h + q], yp),
            send(g.at[1, 0, h + q : TILE], g.at[2, 0, h + q : TILE], ym),
        ]
        if k == 0:
            lay_out(0, 3)
            lay_out(6, 2)
        yield
        arrive(c)
        c = [
            send(g.at[0, :, 0:h], g.at[3, :, 0:h], yp),
            send(g.at[0, :, 0:h], g.at[1, :, 0:h], ym),
            send(g.at[:, 0, h:TILE], g.at[:, 3, h:TILE], xp),
            send(g.at[:, 0, h:TILE], g.at[:, 1, h:TILE], xm),
        ]
        yield
        arrive(c)
        c = [
            send(g.at[3, :, 0:q], g.at[2, :, 0:q], yp),
            send(g.at[1, :, q:h], g.at[2, :, q:h], ym),
            send(g.at[:, 3, h : h + q], g.at[:, 2, h : h + q], xp),
            send(g.at[:, 1, h + q : TILE], g.at[:, 2, h + q : TILE], xm),
        ]
        yield
        arrive(c)

        def slabs(first, last):
            block = gath[k].reshape(ROWS, HC)
            value = f32dot(adj[first * SLAB : last * SLAB, :], block)
            part[k, first:last] = value.reshape(last - first, SLAB, HC)

        top, low = slice(0, HALF), slice(HALF, SLAB)
        slabs(3, 6)
        zsend_p[k, 0, top] = part[k, 4, top].astype(BF16)
        zsend_p[k, 0, low] = part[k, 3, low].astype(BF16)
        zsend_m[k, 0, top] = part[k, 5, top].astype(BF16)
        zsend_m[k, 0, low] = part[k, 4, low].astype(BF16)
        c = [
            send(zsend_p.at[k, 0], zrecv_p.at[k, 0], zp),
            send(zsend_m.at[k, 0], zrecv_m.at[k, 0], zm),
        ]
        slabs(6, 8)
        slabs(0, 3)
        yield
        for s in (1, 2):
            arrive(c)
            rp, rm = zrecv_p.at[k, s - 1], zrecv_m.at[k, s - 1]
            zsend_p[k, s, top] = (part[k, 4 - s, top] + rp[top].astype(F32)).astype(BF16)
            zsend_p[k, s, low] = (part[k, 3 - s, low] + rp[low].astype(F32)).astype(BF16)
            zsend_m[k, s, top] = (part[k, 5 + s, top] + rm[top].astype(F32)).astype(BF16)
            zsend_m[k, s, low] = (part[k, 4 + s, low] + rm[low].astype(F32)).astype(BF16)
            c = [
                send(zsend_p.at[k, s], zrecv_p.at[k, s], zp),
                send(zsend_m.at[k, s], zrecv_m.at[k, s], zm),
            ]
            yield
        arrive(c)
        zsend_p[k, 3, top] = (part[k, 1, top] + zrecv_p[k, 2, top].astype(F32)).astype(BF16)
        zsend_m[k, 3, low] = (part[k, 7, low] + zrecv_m[k, 2, low].astype(F32)).astype(BF16)
        c = [
            send(zsend_p.at[k, 3, top], zrecv_p.at[k, 3, top], zp),
            send(zsend_m.at[k, 3, low], zrecv_m.at[k, 3, low], zm),
        ]
        yield
        arrive(c)
        pre[k, 0, top] = (part[k, 0, top] + zrecv_m[k, 2, top].astype(F32) + zrecv_p[k, 3, top].astype(F32)).astype(BF16)
        pre[k, 0, low] = (part[k, 0, low] + zrecv_p[k, 2, low].astype(F32) + zrecv_m[k, 3, low].astype(F32)).astype(BF16)

        c = [send(pre.at[k, 0], pre.at[k, 7], zp), send(pre.at[k, 0], pre.at[k, 1], zm)]
        if k == 0:
            loads[3].wait()
        activate(k, 0)
        yield
        for s in (1, 2):
            arrive(c)
            c = [
                send(pre.at[k, 8 - s], pre.at[k, 7 - s], zp),
                send(pre.at[k, s], pre.at[k, s + 1], zm),
            ]
            activate(k, 8 - s)
            activate(k, s)
            yield
        arrive(c)
        c = [
            send(pre.at[k, 5, top], pre.at[k, 4, top], zp),
            send(pre.at[k, 3, low], pre.at[k, 4, low], zm),
        ]
        activate(k, 5)
        activate(k, 3)
        yield
        arrive(c)
        activate(k, 4)
        out = pltpu.make_async_copy(layer.at[:, cols], layer_hbm.at[:, cols], out_sem.at[k])
        out.start()
        outs.append(out)

        def columns(i):
            for n in range(2):
                c0 = i * 4 * TILE + n * 2 * TILE
                bpart[k, c0 : c0 + 2 * TILE] = f32dot(adj[:, c0 : c0 + 2 * TILE], delta[k], DN_T)

        def term(i, j, lo, hi):
            c0 = (i * SIDE + j) * TILE
            return bpart[k, c0 + lo : c0 + hi]

        for i in (2, 1, 3, 0):
            columns(i)
        res = yield from together([
            scatter_sum((yp, ym), (xp, xm), lambda a, t, lo, hi: term(a, t, lo, hi),
                        bs1.at[k, 0], bs2.at[k, 0], bs3.at[k, 0], bs4.at[k, 0],
                        br1.at[k, 0], br2.at[k, 0], br3.at[k, 0], br4.at[k, 0], bown.at[k, 0], q),
            scatter_sum((xp, xm), (yp, ym), lambda a, t, lo, hi: term(t, a, h + lo, h + hi),
                        bs1.at[k, 1], bs2.at[k, 1], bs3.at[k, 1], bs4.at[k, 1],
                        br1.at[k, 1], br2.at[k, 1], br3.at[k, 1], br4.at[k, 1], bown.at[k, 1], q),
        ])
        back[k, 0:h] = res[0].astype(BF16)
        back[k, h:TILE] = res[1].astype(BF16)

        wpart[k] = f32dot(feat[...], back[k], DN_T) * ((ROWS * DEPTH) ** -0.5)

        def wterm(i, j, lo, hi):
            start = (((y + i) % SIDE) * SIDE + (x + j) % SIDE) * (INNER // 16) + lo
            return wpart[k, pl.ds(pl.multiple_of(start, 16), hi - lo)]

        flows = [
            scatter_sum((yp, ym), (xp, xm), lambda a, t, lo, hi: wterm(a, t, lo, hi),
                        ws1.at[k, 0], ws2.at[k, 0], ws3.at[k, 0], ws4.at[k, 0],
                        wr1.at[k, 0], wr2.at[k, 0], wr3.at[k, 0], wr4.at[k, 0], wsum.at[k, 0], 16),
            scatter_sum((xp, xm), (yp, ym), lambda a, t, lo, hi: wterm(t, a, 32 + lo, 32 + hi),
                        ws1.at[k, 1], ws2.at[k, 1], ws3.at[k, 1], ws4.at[k, 1],
                        wr1.at[k, 1], wr2.at[k, 1], wr3.at[k, 1], wr4.at[k, 1], wsum.at[k, 1], 16),
        ]
        wflow = together(flows)
        next(wflow)

        mine = f32dot(back[k], weight[pl.ds(pl.multiple_of(f * WIDE, WIDE), WIDE), cols], DN_N)
        theirs = f32dot(back[k], weight[pl.ds(pl.multiple_of((1 - f) * WIDE, WIDE), WIDE), cols], DN_N)
        if k == 0:
            terms[0] = mine
            terms[1] = theirs
        else:
            terms[0] += mine
            terms[1] += theirs
        if k == CHUNKS - 1:
            terms_send[...] = terms[1].astype(BF16)
            swap = send(terms_send, terms_recv, other)
        yield
        res = yield from wflow
        wown[k, 0:32] = res[0]
        wown[k, 32:64] = res[1]
        c = []
        for d in range(1, DEPTH):
            start = pl.multiple_of(((z + d) % DEPTH) * 8, 8)
            c.append(send(wown.at[k, pl.ds(start, 8)], wz.at[k, d], zpeer[d]))
        total = wown[k, pl.ds(pl.multiple_of(z * 8, 8), 8)]
        if k == CHUNKS - 1:
            swap.wait_recv()
            igrad[...] = (terms[0] + terms_recv[...].astype(F32)).astype(BF16)
        yield
        arrive(c)
        for d in range(1, DEPTH):
            total = total + wz[k, d]
        wgrad[:, cols] = total

    outs = []
    flows = {k: flow(k) for k in range(CHUNKS)}
    tick = 0
    while flows:
        for k in sorted(flows):
            if tick >= k * STAGGER:
                try:
                    next(flows[k])
                except StopIteration:
                    del flows[k]
        tick += 1
    for out in outs:
        out.wait()
    for copy in sent:
        copy.wait_send()


def slot_table(coords, count):
    place = coords[:, 0] * (SIDE * SIDE) + coords[:, 1]
    slot = jnp.arange(TILE, dtype=jnp.int32)
    cell = jnp.arange(SIDE * SIDE * SIDE * SIDE, dtype=jnp.int32)
    hit = (place[None, :] == cell[:, None]) & (slot[None, :] < count)
    return jnp.min(jnp.where(hit, slot[None, :], TILE), axis=1)


def on_device(tiles, coords, counts, features, weight, grad_out):
    k2 = (CHUNKS, 2)
    q, w = TILE // 4, 16

    def sums(rows):
        return [
            VMEM((CHUNKS, 2, 2, SIDE, rows, HC), BF16),
            VMEM((CHUNKS, 2, 2, SIDE, 2 * rows, HC), BF16),
            VMEM((CHUNKS, 2, 2, rows, HC), BF16),
            VMEM((CHUNKS, 2, 2, 2 * rows, HC), BF16),
        ]

    scratch = [
        VMEM((TILE + 1, TILE, TILE), BF16),
        VMEM((ROWS, ROWS), BF16),
        VMEM((TILE, INNER), BF16),
        VMEM((INNER, WIDE), BF16),
        VMEM((ROWS, WIDE), BF16),
        VMEM((ROWS, WIDE), BF16),
        VMEM((CHUNKS, SIDE, SIDE, TILE, HC), BF16),
        VMEM((CHUNKS, DEPTH, SLAB, HC), F32),
        VMEM((CHUNKS, 4, SLAB, HC), BF16),
        VMEM((CHUNKS, 4, SLAB, HC), BF16),
        VMEM((CHUNKS, 4, SLAB, HC), BF16),
        VMEM((CHUNKS, 4, SLAB, HC), BF16),
        VMEM((CHUNKS, DEPTH, SLAB, HC), BF16),
        VMEM((CHUNKS, ROWS, HC), BF16),
        VMEM((CHUNKS, ROWS, HC), F32),
        VMEM((CHUNKS, TILE, HC), BF16),
        VMEM((CHUNKS, INNER, HC), F32),
        VMEM((CHUNKS, INNER // 16, HC), F32),
        VMEM((CHUNKS, DEPTH, 8, HC), F32),
        VMEM((2, TILE, WIDE), F32),
        VMEM((TILE, WIDE), BF16),
        VMEM((TILE, WIDE), BF16),
        *sums(q), *sums(q), VMEM((CHUNKS, 2, SIDE, 2 * q, HC), F32),
        *sums(w), *sums(w), VMEM((CHUNKS, 2, SIDE, 2 * w, HC), F32),
        pltpu.SemaphoreType.DMA((4,)),
        pltpu.SemaphoreType.DMA((CHUNKS,)),
        pltpu.SemaphoreType.DMA((71 * CHUNKS + 1,)),
        pltpu.SemaphoreType.DMA((71 * CHUNKS + 1,)),
    ]
    anywhere = pl.BlockSpec(memory_space=pl.ANY)
    return pl.pallas_call(
        kernel,
        out_shape=(
            jax.ShapeDtypeStruct((ROWS, WIDE), BF16),
            jax.ShapeDtypeStruct((8, WIDE), F32),
            jax.ShapeDtypeStruct((TILE, WIDE), BF16),
        ),
        in_specs=[pl.BlockSpec(memory_space=pltpu.SMEM)] + [anywhere] * 4,
        out_specs=(anywhere, pl.BlockSpec(memory_space=VMEM), pl.BlockSpec(memory_space=VMEM)),
        scratch_shapes=scratch,
        compiler_params=pltpu.CompilerParams(
            collective_id=0, has_side_effects=True, vmem_limit_bytes=60 * 1024 * 1024
        ),
        cost_estimate=pl.CostEstimate(flops=9 * 10**9, bytes_accessed=10 * 2**20, transcendentals=2 * 2**20),
        name="graph_layer",
    )(slot_table(coords[0, 0], counts[0, 0]), tiles[0, 0], features, weight, grad_out)


def solution(mesh):
    return jax.shard_map(
        on_device,
        mesh=mesh,
        in_specs=(
            P("row", "col", None, None, None),
            P("row", "col", None, None),
            P("row", "col"),
            P(("col", "row"), None),
            P(None, "feat"),
            P("row", "feat"),
        ),
        out_specs=(P("row", "feat"), P(("row", "col"), "feat"), P(("col", "row"), "feat")),
        check_vma=False,
    )
```

time: 390 us -> 130 us (0.33)
  waiting for transfers between devices: 318 us -> 0 us
  Pallas kernels: 0 us -> 122 us
  matrix products: 25.6 us -> 0 us
  other arithmetic: 15 us -> 1.45 us
  between operations: 14.8 us -> 1.31 us
  local copies, waits for them, and re-layouts: 14.7 us -> 4.35 us
    reduce_scatter x3 -> x0, waiting for transfers between devices: 133 us -> none  [the longest x1 77.6 us: on_device(): lax.psum_scatter(back_partial, 'row', scatter_dimension=0, tiled=True)]
    pallas_call x0 -> x1, Pallas kernels: none -> 122 us  [on_device(): pl.pallas_call(kernel, out_shape=(jax.ShapeDtypeStruct((ROWS, WIDE), BF16...]
    unnamed x9 -> x0, waiting for transfers between devices: 114 us -> none
    all_gather x2 -> x0, waiting for transfers between devices: 71.2 us -> none  [the longest x1 41.7 us: on_device(): pre = lax.all_gather(own, 'col', axis=0, tiled=True).astype(F32)]
    dot_general x5 -> x0, matrix products: 25.6 us -> none  [the longest x1 11.3 us: on_device(): lax.dot_general(dense, delta, (((0,), (0,)), ((), ())), preferred_element...]
    select_n x2 -> x0, other arithmetic: 11.5 us -> none  [the longest x1 11.5 us: densify(): jnp.where(live[:, None, None], tiles[where_from], jnp.zeros((), tiles.dty...]
    gather x1 -> x0, local copies, waits for them, and re-layouts: 10.5 us -> none  [densify(): tiles[where_from]]
  transfers between devices with their start and end apart: 7 -> 0, of which waited for: 7 -> 0; matrix products, arithmetic and copies ran while one was open for 7% -> 0% of each run, Pallas kernels for 0% -> 0%
where the time goes in v2:
time: 130 us; the launch traced here: 129 us
  Pallas kernels  122 us (94%)
  local copies, waits for them, and re-layouts  4.35 us (3%)
  other arithmetic  1.45 us (1%)
  between operations  1.31 us (1%)
    pallas_call x1, Pallas kernels, on_device(): pl.pallas_call(kernel, out_shape=(jax.ShapeDtypeStruct((ROWS, WIDE), BF16...  122 us
    unnamed x7, local copies, waits for them, and re-layouts  4.35 us

profile of v2, /device:TPU:2, one launch (start us, length us, event | category | flops | bytes accessed | tf_op | source)
XLA Modules:
  0.0 129.3 jit_solution(17850180314683550811)
XLA Ops:
  1.3 0.8 add_bitcast_fusion
  2.0 0.7 select_reduce_fusion.slot_of
  2.7 122.2 %graph_layer.1 = (bf16[2048,512]{1,0:T(8,128)(2,1)}, f32[8,512]{1,0:T(8,128)}, bf16[128,512]{1,0:T(8,128)(2,1)}) custom-call(s32[256]{0:T(256)} %select_reduce_fusion.slot_of, bf16[128,128,128]{2,1,0:T(8,128)(2,1)} %bitcast.6, bf16[128,1024]{1,0:T(8,128)(2,1)} %feat_hbm.1, bf16[1024,512]{1,0:T(8,128)(2,1)} %weight_hbm.1, bf16[2048,512]{1,0:T(8,128)(2,1)} %gout_hbm.1), custom_call_target="tpu_custom_call" | custom-call | flops 8999999488 | bytes 10485760 | tf_op jit(solution)/shard_map/graph_layer/pallas_call | solution.py:415
  124.9 0.0 copy-start.1
  124.9 0.0 copy-start
  124.9 3.1 %copy.13 = bf16[2048,512]{1,0:T(8,128)(2,1)} copy(bf16[2048,512]{1,0:T(8,128)(2,1)} %get-tuple-element.6) | data formatting | bytes 4194304
  128.0 0.0 copy-done.1
  128.0 0.6 copy.14
  128.6 0.0 copy-done
  128.6 0.7 copy.15
  (1 shorter events, 0.0 us)
Async XLA Ops:
  124.9 3.1 %copy-start.1 = (f32[8,512]{1,0:T(8,128)S(1)}, f32[8,512]{1,0:T(8,128)}, u32[]{:S(2)}) copy-start(f32[8,512]{1,0:T(8,128)} %get-tuple-element.7) | copy-start | bytes 49156
  124.9 3.7 %copy-start = (bf16[128,512]{1,0:T(8,128)(2,1)S(1)}, bf16[128,512]{1,0:T(8,128)(2,1)}, u32[]{:S(2)}) copy-start(bf16[128,512]{1,0:T(8,128)(2,1)} %get-tuple-element.8) | copy-start | bytes 393220

commit v3 on v1

v3 whole, which is shorter than its diff:
```python
import functools

import jax
import jax.numpy as jnp
from jax import lax
from jax.experimental import pallas as pl
from jax.experimental.pallas import tpu as pltpu
from jax.sharding import PartitionSpec as P

BF16 = jnp.bfloat16
F32 = jnp.float32
MESH = pl.DeviceIdType.MESH
VMEM = pltpu.VMEM

VMEM_LIMIT = 60 * 1024 * 1024
SIDE = 4
DEPTH = 8
TILE = 128
ROWS = 2048
SLAB = ROWS // DEPTH
HALF = SLAB // 2
WIDE = 512
INNER = 1024
WIDTHS = (256, 128, 128)
PARTS = len(WIDTHS)
ORDER = (
    0, 9, 1, 0, 1, 0, 1, 2, 0, 1, 2, 9, 0, 2, 1, 0, 2, 9, 1, 2, 0, 9, 2, 0, 1, 0, 1, 9, 2, 0,
    2, 1, 0, 1, 2, 9, 0, 1, 2, 0, 3, 6, 1, 2, 3, 1, 4, 6, 7, 2, 3, 4, 2, 5, 8, 7, 3, 6, 4, 8,
    5, 7, 8, 6, 4, 3, 5, 7, 8, 4, 6, 5, 7, 8, 5, 7, 8, 6, 5,
)
FIRST = [sum(WIDTHS[:k]) for k in range(len(WIDTHS))]
LAST = PARTS - 1
SLOTS = 21

DN_T = (((0,), (0,)), ((), ()))
DN_N = (((1,), (1,)), ((), ()))


def f32dot(a, b, dims=(((1,), (0,)), ((), ()))):
    return lax.dot_general(a, b, dims, preferred_element_type=F32)


def kernel(names, slot_of, tiles_hbm, feat_hbm, weight_hbm, gout_hbm, layer_hbm, wgrad, igrad, *refs):
    r = dict(zip(names, refs))
    tiles, adj, feat, weight, gout, layer = (r[n] for n in ("tiles", "adj", "feat", "weight", "gout", "layer"))
    nodes, terms, terms_send, terms_recv = (r[n] for n in ("nodes", "terms", "terms_send", "terms_recv"))
    local_sem, out_sem, send_sem, recv_sem = (r[n] for n in ("local_sem", "out_sem", "send_sem", "recv_sem"))
    row = lax.axis_index("row")
    z = lax.axis_index("col")
    f = lax.axis_index("feat")
    y, x = row // SIDE, row % SIDE

    def at(dy, dx, dz):
        return (((y + dy + SIDE) % SIDE) * SIDE + (x + dx + SIDE) % SIDE, (z + dz + DEPTH) % DEPTH, f)

    xp, xm = at(0, 1, 0), at(0, -1, 0)
    yp, ym = at(1, 0, 0), at(-1, 0, 0)
    ways = [xp, xm, yp, ym]
    zpeer = [None] + [at(0, 0, d) for d in range(1, DEPTH)]
    zp, zm = zpeer[1], zpeer[DEPTH - 1]
    other = (row, z, 1 - f)

    def weight_load(k):
        cols = slice(FIRST[k], FIRST[k] + WIDTHS[k])
        return pltpu.make_async_copy(weight_hbm.at[:, cols], weight.at[:, cols], local_sem.at[3 + k])

    loads = [
        pltpu.make_async_copy(feat_hbm, feat, local_sem.at[0]),
        weight_load(0),
        pltpu.make_async_copy(tiles_hbm, tiles.at[0:TILE], local_sem.at[1]),
        *[weight_load(k) for k in range(1, LAST + 1)],
        pltpu.make_async_copy(gout_hbm, gout, local_sem.at[2]),
    ]
    for load in loads:
        load.start()

    barrier = pltpu.get_barrier_semaphore()
    partners = [xp, xm, yp, ym, other] + zpeer[1:]
    for device in partners:
        pl.semaphore_signal(barrier, inc=1, device_id=device, device_id_type=MESH)

    def send(src, dst, to, slot):
        copy = pltpu.make_async_remote_copy(
            src_ref=src, dst_ref=dst, send_sem=send_sem.at[slot], recv_sem=recv_sem.at[slot],
            device_id=to, device_id_type=MESH,
        )
        copy.start()
        return copy

    def arrive(copies):
        for copy in copies:
            copy.wait_recv()
        for copy in copies:
            copy.wait_send()

    def lay_out(first, count):
        def one(n, carry):
            slab = first + n // 2
            tile_row = ((z + slab) % DEPTH) * 2 + n % 2
            start = pl.multiple_of((slab * 2 + n % 2) * TILE, TILE)
            for i in range(SIDE):
                for j in range(SIDE):
                    tile_col = ((y + i) % SIDE) * SIDE + (x + j) % SIDE
                    slot = slot_of[tile_row * SIDE * SIDE + tile_col]
                    c = (i * SIDE + j) * TILE
                    adj[pl.ds(start, TILE), c : c + TILE] = tiles[slot]
            return carry

        lax.fori_loop(0, 2 * count, one, 0)

    def scatter_sum(term, bufs, q, slot):
        s1, s2, s3, s4, r1, r2, r3, r4, own = bufs
        first, last = ((2, 3), (0, 1)), ((0, 1), (2, 3))

        def acc(side, a, t, lo, hi):
            return term(a, t, lo, hi) if side == 0 else term(t, a, 2 * q + lo, 2 * q + hi)

        def send_all(src, dst, to, phase):
            return [
                send(src.at[n, d], dst.at[n, d], ways[to[n][d]], slot + 2 * to[n][d] + phase % 2)
                for n in range(2)
                for d in range(2)
            ]

        for n in range(2):
            for t in range(SIDE):
                s1[n, 0, t] = acc(n, 2, t, 0, q).astype(BF16)
                s1[n, 1, t] = acc(n, 2, t, q, 2 * q).astype(BF16)
        c = send_all(s1, r1, first, 0)
        yield
        arrive(c)
        for n in range(2):
            for t in range(SIDE):
                s2[n, 0, t, 0:q] = (acc(n, 1, t, 0, q) + r1[n, 0, t].astype(F32)).astype(BF16)
                s2[n, 0, t, q : 2 * q] = acc(n, 1, t, q, 2 * q).astype(BF16)
                s2[n, 1, t, 0:q] = acc(n, 3, t, 0, q).astype(BF16)
                s2[n, 1, t, q : 2 * q] = (acc(n, 3, t, q, 2 * q) + r1[n, 1, t].astype(F32)).astype(BF16)
        c = send_all(s2, r2, first, 1)
        yield
        arrive(c)

        def add(n, t):
            own[n, t] = acc(n, 0, t, 0, 2 * q) + r2[n, 0, t].astype(F32) + r2[n, 1, t].astype(F32)

        for n in range(2):
            add(n, 2)
            s3[n, 0] = own[n, 2, 0:q].astype(BF16)
            s3[n, 1] = own[n, 2, q : 2 * q].astype(BF16)
        c = send_all(s3, r3, last, 2)
        for n in range(2):
            for t in (1, 3, 0):
                add(n, t)
        yield
        arrive(c)
        for n in range(2):
            s4[n, 0, 0:q] = (own[n, 1, 0:q] + r3[n, 0].astype(F32)).astype(BF16)
            s4[n, 0, q : 2 * q] = own[n, 1, q : 2 * q].astype(BF16)
            s4[n, 1, 0:q] = own[n, 3, 0:q].astype(BF16)
            s4[n, 1, q : 2 * q] = (own[n, 3, q : 2 * q] + r3[n, 1].astype(F32)).astype(BF16)
        c = send_all(s4, r4, last, 3)
        yield
        arrive(c)
        return [own[n, 0] + r4[n, 0].astype(F32) + r4[n, 1].astype(F32) for n in range(2)]

    def plane_gather(g, slot):
        h, q = TILE // 2, TILE // 4

        def send_all(phase, *moves):
            return [
                send(src, dst, to, slot + 2 * n + phase % 2)
                for n, (src, dst, to) in enumerate(zip(moves[0::2], moves[1::2], (xp, xm, yp, ym)))
            ]

        own_h, own_l = g.at[0, 0, 0:h], g.at[0, 0, h:TILE]
        c = send_all(
            0, own_h, g.at[0, 3, 0:h], own_h, g.at[0, 1, 0:h],
            own_l, g.at[3, 0, h:TILE], own_l, g.at[1, 0, h:TILE],
        )
        yield
        arrive(c)
        c = send_all(
            1, g.at[0, 3, 0:q], g.at[0, 2, 0:q], g.at[0, 1, q:h], g.at[0, 2, q:h],
            g.at[3, 0, h : h + q], g.at[2, 0, h : h + q], g.at[1, 0, h + q : TILE], g.at[2, 0, h + q : TILE],
        )
        yield
        arrive(c)
        c = send_all(
            2, g.at[:, 0, h:TILE], g.at[:, 3, h:TILE], g.at[:, 0, h:TILE], g.at[:, 1, h:TILE],
            g.at[0, :, 0:h], g.at[3, :, 0:h], g.at[0, :, 0:h], g.at[1, :, 0:h],
        )
        yield
        arrive(c)
        c = send_all(
            3, g.at[:, 3, h : h + q], g.at[:, 2, h : h + q], g.at[:, 1, h + q : TILE], g.at[:, 2, h + q : TILE],
            g.at[3, :, 0:q], g.at[2, :, 0:q], g.at[1, :, q:h], g.at[2, :, q:h],
        )
        yield
        arrive(c)

    def gather_features():
        mine = nodes.at[f]
        for n in range(2):

            @pl.when(f == n)
            def _():
                nodes[n, 0, 0] = feat[:, n * WIDE : (n + 1) * WIDE]

        yield from plane_gather(mine, SLOTS * PARTS)
        c = [send(mine, nodes.at[f], other, SLOTS * PARTS + 8)]
        yield
        arrive(c)

    def flow(k):
        hc, slot = WIDTHS[k], SLOTS * k
        cols = slice(FIRST[k], FIRST[k] + hc)
        g, part, pre, delta, bsum, bpart = (r[n + str(k)] for n in ("gath", "part", "pre", "delta", "bsum", "bpart"))
        zsend_p, zsend_m, zrecv_p, zrecv_m = (r[n + str(k)] for n in ("zsend_p", "zsend_m", "zrecv_p", "zrecv_m"))

        if k == 0:
            loads[0].wait()
        loads[1 if k == 0 else 2 + k].wait()
        g[0, 0] = f32dot(feat[...], weight[:, cols]).astype(BF16)
        if k == 0:
            pl.semaphore_wait(barrier, len(partners))
        gather = plane_gather(g, slot)
        next(gather)
        if k == 0:
            loads[2].wait()
            tiles[TILE] = jnp.zeros((TILE, TILE), BF16)
            lay_out(3, 3)
        yield
        next(gather)
        if k == 0:
            lay_out(0, 3)
            lay_out(6, 2)
        yield
        yield from gather

        def slabs(first, last):
            value = f32dot(adj[first * SLAB : last * SLAB, :], g[...].reshape(ROWS, hc))
            part[first:last] = value.reshape(last - first, SLAB, hc)

        def send_z(step, up, down):
            return [send(*up, zp, slot + 16 + step % 2), send(*down, zm, slot + 18 + step % 2)]

        top, low = slice(0, HALF), slice(HALF, SLAB)
        slabs(3, 6)
        zsend_p[0, top] = part[4, top].astype(BF16)
        zsend_p[0, low] = part[3, low].astype(BF16)
        zsend_m[0, top] = part[5, top].astype(BF16)
        zsend_m[0, low] = part[4, low].astype(BF16)
        c = send_z(0, (zsend_p.at[0], zrecv_p.at[0]), (zsend_m.at[0], zrecv_m.at[0]))
        slabs(6, 8)
        slabs(0, 3)
        yield
        for s in (1, 2):
            arrive(c)
            zsend_p[s, top] = (part[4 - s, top] + zrecv_p[s - 1, top].astype(F32)).astype(BF16)
            zsend_p[s, low] = (part[3 - s, low] + zrecv_p[s - 1, low].astype(F32)).astype(BF16)
            zsend_m[s, top] = (part[5 + s, top] + zrecv_m[s - 1, top].astype(F32)).astype(BF16)
            zsend_m[s, low] = (part[4 + s, low] + zrecv_m[s - 1, low].astype(F32)).astype(BF16)
            c = send_z(s, (zsend_p.at[s], zrecv_p.at[s]), (zsend_m.at[s], zrecv_m.at[s]))
            yield
        arrive(c)
        zsend_p[3, top] = (part[1, top] + zrecv_p[2, top].astype(F32)).astype(BF16)
        zsend_m[3, low] = (part[7, low] + zrecv_m[2, low].astype(F32)).astype(BF16)
        c = send_z(3, (zsend_p.at[3, top], zrecv_p.at[3, top]), (zsend_m.at[3, low], zrecv_m.at[3, low]))
        yield
        arrive(c)
        pre[0, top] = (part[0, top] + zrecv_m[2, top].astype(F32) + zrecv_p[3, top].astype(F32)).astype(BF16)
        pre[0, low] = (part[0, low] + zrecv_p[2, low].astype(F32) + zrecv_m[3, low].astype(F32)).astype(BF16)

        def activate(i):
            start = pl.multiple_of(((z + i) % DEPTH) * SLAB, SLAB)
            value = pre[i].astype(F32)
            sig = 0.5 + 0.5 * jnp.tanh(0.5 * value)
            layer[pl.ds(start, SLAB), cols] = (value * sig).astype(BF16)
            slope = sig * (1.0 + value * (1.0 - sig))
            delta[i * SLAB : (i + 1) * SLAB] = (gout[pl.ds(start, SLAB), cols].astype(F32) * slope).astype(BF16)

        c = send_z(4, (pre.at[0], pre.at[7]), (pre.at[0], pre.at[1]))
        if k == 0:
            loads[-1].wait()
        activate(0)
        yield
        for s in (1, 2):
            arrive(c)
            c = send_z(4 + s, (pre.at[8 - s], pre.at[7 - s]), (pre.at[s], pre.at[s + 1]))
            activate(8 - s)
            activate(s)
            yield
        arrive(c)
        c = send_z(7, (pre.at[5, top], pre.at[4, top]), (pre.at[3, low], pre.at[4, low]))
        activate(5)
        activate(3)
        for n in range(DEPTH):
            c0 = n * SLAB
            bsum[c0 : c0 + SLAB] = f32dot(adj[0 : 4 * SLAB, c0 : c0 + SLAB], delta[0 : 4 * SLAB], DN_T) + f32dot(
                adj[5 * SLAB :, c0 : c0 + SLAB], delta[5 * SLAB :], DN_T
            )
        yield
        arrive(c)
        activate(4)
        mid = slice(4 * SLAB, 5 * SLAB)
        for n in (4, 5, 0, 1, 2, 3, 6, 7):
            c0 = n * SLAB
            value = bsum[c0 : c0 + SLAB] + f32dot(adj[mid, c0 : c0 + SLAB], delta[mid], DN_T)
            bpart[n // 2, n % 2 * 2 : n % 2 * 2 + 2] = value.astype(BF16).reshape(2, TILE, hc)
        out = pltpu.make_async_copy(layer.at[:, cols], layer_hbm.at[:, cols], out_sem.at[k])
        out.start()
        outs.append(out)

    def sum_back(k):
        hc = WIDTHS[k]
        cols = slice(FIRST[k], FIRST[k] + hc)
        bpart, back = r["bpart" + str(k)], r["back" + str(k)]

        def term(i, j, lo, hi):
            return bpart[i, j, lo:hi].astype(F32)

        res = yield from scatter_sum(term, sum_refs("b", k), TILE // 4, SLOTS * k)
        back[0 : TILE // 2] = res[0].astype(BF16)
        back[TILE // 2 : TILE] = res[1].astype(BF16)
        theirs = f32dot(back[...], weight[pl.ds(pl.multiple_of((1 - f) * WIDE, WIDE), WIDE), cols], DN_N)
        if k > 0:
            theirs += terms[1]
        if k < LAST:
            terms[1] = theirs
        else:
            terms_send[...] = theirs.astype(BF16)
            swap = [send(terms_send, terms_recv, other, SLOTS * PARTS + 9)]
        mine = f32dot(back[...], weight[pl.ds(pl.multiple_of(f * WIDE, WIDE), WIDE), cols], DN_N)
        if k > 0:
            mine += terms[0]
        terms[0] = mine
        if k == LAST:
            yield
            arrive(swap)
            igrad[...] = (terms[0] + terms_recv[...].astype(F32)).astype(BF16)

    def sum_weight(k):
        hc = WIDTHS[k]
        cols = slice(FIRST[k], FIRST[k] + hc)
        bpart, wpart, wown, wz = (r[n + str(k)] for n in ("bpart", "wpart", "wown", "wz"))
        block = bpart[...].reshape(ROWS, hc)
        for n in range(2):
            value = f32dot(nodes[n].reshape(ROWS, WIDE), block, DN_T)
            wpart[n * WIDE : (n + 1) * WIDE] = value * ((ROWS * DEPTH) ** -0.5)

        def term(i, j, lo, hi):
            start = (((y + i) % SIDE) * SIDE + (x + j) % SIDE) * (INNER // 16) + lo
            return wpart[pl.ds(pl.multiple_of(start, 16), hi - lo)]

        res = yield from scatter_sum(term, sum_refs("w", k), 16, SLOTS * k + 8)
        wown[0:32] = res[0]
        wown[32:64] = res[1]
        slot = SLOTS * k + 20
        for d in range(1, DEPTH):
            start = pl.multiple_of(((z + d) % DEPTH) * 8, 8)
            send(wown.at[pl.ds(start, 8)], wz.at[d], zpeer[d], slot)
        yield
        others = wz.at[1:DEPTH]
        pltpu.make_async_copy(others, others, recv_sem.at[slot]).wait()
        pltpu.make_async_copy(others, others, send_sem.at[slot]).wait()
        total = wown[pl.ds(pl.multiple_of(z * 8, 8), 8)]
        for d in range(1, DEPTH):
            total = total + wz[d]
        wgrad[:, cols] = total

    def sum_refs(kind, k):
        return [r[kind + n + str(k)] for n in ("s1", "s2", "s3", "s4", "r1", "r2", "r3", "r4", "acc")]

    outs = []
    flows = [make(k) for make in (flow, sum_back, sum_weight) for k in range(PARTS)] + [gather_features()]
    for n in ORDER:
        next(flows[n], None)
    for out in outs:
        out.wait()


def slot_table(coords, count):
    place = coords[:, 0] * (SIDE * SIDE) + coords[:, 1]
    slot = jnp.arange(TILE, dtype=jnp.int32)
    cell = jnp.arange(SIDE * SIDE * SIDE * SIDE, dtype=jnp.int32)
    hit = (place[None, :] == cell[:, None]) & (slot[None, :] < count)
    return jnp.min(jnp.where(hit, slot[None, :], TILE), axis=1)


def scratch_of():
    dma = pltpu.SemaphoreType.DMA
    slots = SLOTS * PARTS + 10
    refs = {
        "tiles": VMEM((TILE + 1, TILE, TILE), BF16),
        "adj": VMEM((ROWS, ROWS), BF16),
        "feat": VMEM((TILE, INNER), BF16),
        "weight": VMEM((INNER, WIDE), BF16),
        "gout": VMEM((ROWS, WIDE), BF16),
        "layer": VMEM((ROWS, WIDE), BF16),
        "nodes": VMEM((2, SIDE, SIDE, TILE, WIDE), BF16),
        "terms": VMEM((2, TILE, WIDE), F32),
        "terms_send": VMEM((TILE, WIDE), BF16),
        "terms_recv": VMEM((TILE, WIDE), BF16),
        "local_sem": dma((3 + len(WIDTHS),)),
        "out_sem": dma((len(WIDTHS),)),
        "send_sem": dma((slots,)),
        "recv_sem": dma((slots,)),
    }
    for k, hc in enumerate(WIDTHS):
        shapes = {
            "gath": ((SIDE, SIDE, TILE, hc), BF16),
            "part": ((DEPTH, SLAB, hc), F32),
            "zsend_p": ((4, SLAB, hc), BF16),
            "zsend_m": ((4, SLAB, hc), BF16),
            "zrecv_p": ((4, SLAB, hc), BF16),
            "zrecv_m": ((4, SLAB, hc), BF16),
            "pre": ((DEPTH, SLAB, hc), BF16),
            "delta": ((ROWS, hc), BF16),
            "bsum": ((ROWS, hc), F32),
            "bpart": ((SIDE, SIDE, TILE, hc), BF16),
            "back": ((TILE, hc), BF16),
            "wpart": ((INNER, hc), F32),
            "wown": ((INNER // 16, hc), F32),
            "wz": ((DEPTH, 8, hc), F32),
        }
        for kind, q in (("b", TILE // 4), ("w", INNER // 64)):
            for way in "sr":
                shapes[kind + way + "1"] = ((2, 2, SIDE, q, hc), BF16)
                shapes[kind + way + "2"] = ((2, 2, SIDE, 2 * q, hc), BF16)
                shapes[kind + way + "3"] = ((2, 2, q, hc), BF16)
                shapes[kind + way + "4"] = ((2, 2, 2 * q, hc), BF16)
            shapes[kind + "acc"] = ((2, SIDE, 2 * q, hc), F32)
        for name, (shape, dtype) in shapes.items():
            refs[name + str(k)] = VMEM(shape, dtype)
    return refs


def on_device(tiles, coords, counts, features, weight, grad_out):
    scratch = scratch_of()
    anywhere = pl.BlockSpec(memory_space=pl.ANY)
    shapes = (
        jax.ShapeDtypeStruct((ROWS, WIDE), BF16),
        jax.ShapeDtypeStruct((8, WIDE), F32),
        jax.ShapeDtypeStruct((TILE, WIDE), BF16),
    )
    return pl.pallas_call(
        functools.partial(kernel, tuple(scratch)),
        out_shape=shapes,
        in_specs=[pl.BlockSpec(memory_space=pltpu.SMEM)] + [anywhere] * 4,
        out_specs=(anywhere, pl.BlockSpec(memory_space=VMEM), pl.BlockSpec(memory_space=VMEM)),
        scratch_shapes=list(scratch.values()),
        compiler_params=pltpu.CompilerParams(
            collective_id=0, has_side_effects=True, vmem_limit_bytes=VMEM_LIMIT
        ),
        cost_estimate=pl.CostEstimate(flops=11 * 10**9, bytes_accessed=10 * 2**20, transcendentals=2**20),
        name="graph_layer",
    )(slot_table(coords[0, 0], counts[0, 0]), tiles[0, 0], features, weight, grad_out)

def solution(mesh):
    return jax.shard_map(
        on_device,
        mesh=mesh,
        in_specs=(
            P("row", "col", None, None, None),
            P("row", "col", None, None),
            P("row", "col"),
            P(("col", "row"), None),
            P(None, "feat"),
            P("row", "feat"),
        ),
        out_specs=(P("row", "feat"), P(("row", "col"), "feat"), P(("col", "row"), "feat")),
        check_vma=False,
    )
```

time: 390 us -> 112 us (0.29)
  waiting for transfers between devices: 318 us -> 0 us
  Pallas kernels: 0 us -> 104 us
  matrix products: 25.6 us -> 0 us
  other arithmetic: 15 us -> 1.45 us
  between operations: 14.8 us -> 1.31 us
  local copies, waits for them, and re-layouts: 14.7 us -> 4.35 us
    reduce_scatter x3 -> x0, waiting for transfers between devices: 133 us -> none  [the longest x1 77.6 us: on_device(): lax.psum_scatter(back_partial, 'row', scatter_dimension=0, tiled=True)]
    unnamed x9 -> x0, waiting for transfers between devices: 114 us -> none
    pallas_call x0 -> x1, Pallas kernels: none -> 104 us  [on_device(): pl.pallas_call(functools.partial(kernel, tuple(scratch)), out_shape=shape...]
    all_gather x2 -> x0, waiting for transfers between devices: 71.2 us -> none  [the longest x1 41.7 us: on_device(): pre = lax.all_gather(own, 'col', axis=0, tiled=True).astype(F32)]
    dot_general x5 -> x0, matrix products: 25.6 us -> none  [the longest x1 11.3 us: on_device(): lax.dot_general(dense, delta, (((0,), (0,)), ((), ())), preferred_element...]
    select_n x2 -> x0, other arithmetic: 11.5 us -> none  [the longest x1 11.5 us: densify(): jnp.where(live[:, None, None], tiles[where_from], jnp.zeros((), tiles.dty...]
    gather x1 -> x0, local copies, waits for them, and re-layouts: 10.5 us -> none  [densify(): tiles[where_from]]
  transfers between devices with their start and end apart: 7 -> 0, of which waited for: 7 -> 0; matrix products, arithmetic and copies ran while one was open for 7% -> 0% of each run, Pallas kernels for 0% -> 0%
where the time goes in v3:
time: 112 us; the launch traced here: 111 us
  Pallas kernels  104 us (93%)
  local copies, waits for them, and re-layouts  4.35 us (4%)
  other arithmetic  1.45 us (1%)
  between operations  1.31 us (1%)
    pallas_call x1, Pallas kernels, on_device(): pl.pallas_call(functools.partial(kernel, tuple(scratch)), out_shape=shape...  104 us
    unnamed x7, local copies, waits for them, and re-layouts  4.35 us

profile of v3, /device:TPU:2, one launch (start us, length us, event | category | flops | bytes accessed | tf_op | source)
XLA Modules:
  0.0 111.4 jit_solution(12858401406211978751)
XLA Ops:
  1.3 0.8 add_bitcast_fusion
  2.0 0.7 select_reduce_fusion.slot_of
  2.7 104.3 %graph_layer.1 = (bf16[2048,512]{1,0:T(8,128)(2,1)}, f32[8,512]{1,0:T(8,128)}, bf16[128,512]{1,0:T(8,128)(2,1)}) custom-call(s32[256]{0:T(256)} %select_reduce_fusion.slot_of, bf16[128,128,128]{2,1,0:T(8,128)(2,1)} %bitcast.6, bf16[128,1024]{1,0:T(8,128)(2,1)} %feat_hbm.1, bf16[1024,512]{1,0:T(8,128)(2,1)} %weight_hbm.1, bf16[2048,512]{1,0:T(8,128)(2,1)} %gout_hbm.1), custom_call_target="tpu_custom_call" | custom-call | flops 11000000512 | bytes 10485760 | tf_op jit(solution)/shard_map/graph_layer/pallas_call | solution.py:445
  107.0 0.0 copy-start.1
  107.0 0.0 copy-start
  107.0 3.1 %copy.13 = bf16[2048,512]{1,0:T(8,128)(2,1)} copy(bf16[2048,512]{1,0:T(8,128)(2,1)} %get-tuple-element.6) | data formatting | bytes 4194304
  110.1 0.0 copy-done.1
  110.1 0.6 copy.14
  110.7 0.0 copy-done
  110.7 0.7 copy.15
  (1 shorter events, 0.0 us)
Async XLA Ops:
  107.0 3.1 %copy-start.1 = (f32[8,512]{1,0:T(8,128)S(1)}, f32[8,512]{1,0:T(8,128)}, u32[]{:S(2)}) copy-start(f32[8,512]{1,0:T(8,128)} %get-tuple-element.7) | copy-start | bytes 49156
  107.0 3.7 %copy-start = (bf16[128,512]{1,0:T(8,128)(2,1)S(1)}, bf16[128,512]{1,0:T(8,128)(2,1)}, u32[]{:S(2)}) copy-start(bf16[128,512]{1,0:T(8,128)(2,1)} %get-tuple-element.8) | copy-start | bytes 393220

commit v4 on v3

--- a/solution.py
+++ b/solution.py
@@ -12,7 +12,7 @@
 MESH = pl.DeviceIdType.MESH
 VMEM = pltpu.VMEM
 
-VMEM_LIMIT = 60 * 1024 * 1024
+VMEM_LIMIT = 50 * 1024 * 1024
 SIDE = 4
 DEPTH = 8
 TILE = 128
@@ -21,16 +21,15 @@
 HALF = SLAB // 2
 WIDE = 512
 INNER = 1024
-WIDTHS = (256, 128, 128)
+WIDTHS = (256, 256)
 PARTS = len(WIDTHS)
 ORDER = (
-    0, 9, 1, 0, 1, 0, 1, 2, 0, 1, 2, 9, 0, 2, 1, 0, 2, 9, 1, 2, 0, 9, 2, 0, 1, 0, 1, 9, 2, 0,
-    2, 1, 0, 1, 2, 9, 0, 1, 2, 0, 3, 6, 1, 2, 3, 1, 4, 6, 7, 2, 3, 4, 2, 5, 8, 7, 3, 6, 4, 8,
-    5, 7, 8, 6, 4, 3, 5, 7, 8, 4, 6, 5, 7, 8, 5, 7, 8, 6, 5,
+    0, 1, 0, 1, 0, 1, 0, 4, 1, 0, 1, 0, 1, 4, 0, 4, 1, 0, 1, 0, 1, 4, 0, 4, 1, 0, 1, 0, 1, 4,
+    0, 2, 1, 3, 2, 3, 2, 3, 2, 3, 2, 3, 5,
 )
 FIRST = [sum(WIDTHS[:k]) for k in range(len(WIDTHS))]
 LAST = PARTS - 1
-SLOTS = 21
+SLOTS = 12
 
 DN_T = (((0,), (0,)), ((), ()))
 DN_N = (((1,), (1,)), ((), ()))
@@ -40,10 +39,12 @@
     return lax.dot_general(a, b, dims, preferred_element_type=F32)
 
 
-def kernel(names, slot_of, tiles_hbm, feat_hbm, weight_hbm, gout_hbm, layer_hbm, wgrad, igrad, *refs):
+def kernel(names, counts, coords_hbm, tiles_hbm, feat_hbm, weight_hbm, gout_hbm, layer_hbm, wgrad, igrad, *refs):
     r = dict(zip(names, refs))
     tiles, adj, feat, weight, gout, layer = (r[n] for n in ("tiles", "adj", "feat", "weight", "gout", "layer"))
-    nodes, terms, terms_send, terms_recv = (r[n] for n in ("nodes", "terms", "terms_send", "terms_recv"))
+    nodes, back, wown, wz, terms_send, terms_recv, table, slot_of = (
+        r[n] for n in ("nodes", "back", "wown", "wz", "terms_send", "terms_recv", "table", "slot_of")
+    )
     local_sem, out_sem, send_sem, recv_sem = (r[n] for n in ("local_sem", "out_sem", "send_sem", "recv_sem"))
     row = lax.axis_index("row")
     z = lax.axis_index("col")
@@ -64,6 +65,8 @@
         cols = slice(FIRST[k], FIRST[k] + WIDTHS[k])
         return pltpu.make_async_copy(weight_hbm.at[:, cols], weight.at[:, cols], local_sem.at[3 + k])
 
+    coords = r["coords"]
+    places = pltpu.make_async_copy(coords_hbm, coords, local_sem.at[4 + PARTS])
     loads = [
         pltpu.make_async_copy(feat_hbm, feat, local_sem.at[0]),
         weight_load(0),
@@ -73,6 +76,7 @@
     ]
     for load in loads:
         load.start()
+    places.start()
 
     barrier = pltpu.get_barrier_semaphore()
     partners = [xp, xm, yp, ym, other] + zpeer[1:]
@@ -92,6 +96,15 @@
             copy.wait_recv()
         for copy in copies:
             copy.wait_send()
+
+    def find_slots():
+        shape = (SIDE**4, TILE)
+        slot = lax.broadcasted_iota(jnp.int32, shape, 1)
+        place = jnp.broadcast_to(coords[0:1] * SIDE**2 + coords[1:2], shape)
+        hit = (place == lax.broadcasted_iota(jnp.int32, shape, 0)) & (slot < counts[0, 0])
+        found = jnp.where(hit, slot, TILE)
+        table[...] = jnp.min(found.T, axis=0, keepdims=True)
+        return pltpu.make_async_copy(table, slot_of, local_sem.at[3 + PARTS])
 
     def lay_out(first, count):
         def one(n, carry):
@@ -101,19 +114,16 @@
             for i in range(SIDE):
                 for j in range(SIDE):
                     tile_col = ((y + i) % SIDE) * SIDE + (x + j) % SIDE
-                    slot = slot_of[tile_row * SIDE * SIDE + tile_col]
+                    slot = slot_of[0, tile_row * SIDE * SIDE + tile_col]
                     c = (i * SIDE + j) * TILE
                     adj[pl.ds(start, TILE), c : c + TILE] = tiles[slot]
             return carry
 
         lax.fori_loop(0, 2 * count, one, 0)
 
-    def scatter_sum(term, bufs, q, slot):
+    def scatter_sum(kinds, bufs, slot):
         s1, s2, s3, s4, r1, r2, r3, r4, own = bufs
         first, last = ((2, 3), (0, 1)), ((0, 1), (2, 3))
-
-        def acc(side, a, t, lo, hi):
-            return term(a, t, lo, hi) if side == 0 else term(t, a, 2 * q + lo, 2 * q + hi)
 
         def send_all(src, dst, to, phase):
             return [
@@ -122,45 +132,60 @@
                 for d in range(2)
             ]
 
-        for n in range(2):
+        def each():
+            at_q = 0
+            for term, q in kinds:
+                for n in range(2):
+
+                    def acc(a, t, lo, hi, n=n, term=term, q=q):
+                        return term(a, t, lo, hi) if n == 0 else term(t, a, 2 * q + lo, 2 * q + hi)
+
+                    one, two = slice(at_q, at_q + q), slice(2 * at_q, 2 * (at_q + q))
+                    yield n, acc, q, one, two, slice(two.start, two.start + q), slice(two.start + q, two.stop)
+                at_q += q
+
+        for n, acc, q, one, two, up, down in each():
             for t in range(SIDE):
-                s1[n, 0, t] = acc(n, 2, t, 0, q).astype(BF16)
-                s1[n, 1, t] = acc(n, 2, t, q, 2 * q).astype(BF16)
+                s1[n, 0, t, one] = acc(2, t, 0, q).astype(BF16)
+                s1[n, 1, t, one] = acc(2, t, q, 2 * q).astype(BF16)
         c = send_all(s1, r1, first, 0)
         yield
         arrive(c)
-        for n in range(2):
+        for n, acc, q, one, two, up, down in each():
             for t in range(SIDE):
-                s2[n, 0, t, 0:q] = (acc(n, 1, t, 0, q) + r1[n, 0, t].astype(F32)).astype(BF16)
-                s2[n, 0, t, q : 2 * q] = acc(n, 1, t, q, 2 * q).astype(BF16)
-                s2[n, 1, t, 0:q] = acc(n, 3, t, 0, q).astype(BF16)
-                s2[n, 1, t, q : 2 * q] = (acc(n, 3, t, q, 2 * q) + r1[n, 1, t].astype(F32)).astype(BF16)
+                s2[n, 0, t, up] = (acc(1, t, 0, q) + r1[n, 0, t, one].astype(F32)).astype(BF16)
+                s2[n, 0, t, down] = acc(1, t, q, 2 * q).astype(BF16)
+                s2[n, 1, t, up] = acc(3, t, 0, q).astype(BF16)
+                s2[n, 1, t, down] = (acc(3, t, q, 2 * q) + r1[n, 1, t, one].astype(F32)).astype(BF16)
         c = send_all(s2, r2, first, 1)
         yield
         arrive(c)
 
-        def add(n, t):
-            own[n, t] = acc(n, 0, t, 0, 2 * q) + r2[n, 0, t].astype(F32) + r2[n, 1, t].astype(F32)
-
-        for n in range(2):
-            add(n, 2)
-            s3[n, 0] = own[n, 2, 0:q].astype(BF16)
-            s3[n, 1] = own[n, 2, q : 2 * q].astype(BF16)
+        def add(t):
+            for n, acc, q, one, two, up, down in each():
+                own[n, t, two] = acc(0, t, 0, 2 * q) + r2[n, 0, t, two].astype(F32) + r2[n, 1, t, two].astype(F32)
+
+        add(2)
+        for n, acc, q, one, two, up, down in each():
+            s3[n, 0, one] = own[n, 2, up].astype(BF16)
+            s3[n, 1, one] = own[n, 2, down].astype(BF16)
         c = send_all(s3, r3, last, 2)
-        for n in range(2):
-            for t in (1, 3, 0):
-                add(n, t)
-        yield
-        arrive(c)
-        for n in range(2):
-            s4[n, 0, 0:q] = (own[n, 1, 0:q] + r3[n, 0].astype(F32)).astype(BF16)
-            s4[n, 0, q : 2 * q] = own[n, 1, q : 2 * q].astype(BF16)
-            s4[n, 1, 0:q] = own[n, 3, 0:q].astype(BF16)
-            s4[n, 1, q : 2 * q] = (own[n, 3, q : 2 * q] + r3[n, 1].astype(F32)).astype(BF16)
+        for t in (1, 3, 0):
+            add(t)
+        yield
+        arrive(c)
+        for n, acc, q, one, two, up, down in each():
+            s4[n, 0, up] = (own[n, 1, up] + r3[n, 0, one].astype(F32)).astype(BF16)
+            s4[n, 0, down] = own[n, 1, down].astype(BF16)
+            s4[n, 1, up] = own[n, 3, up].astype(BF16)
+            s4[n, 1, down] = (own[n, 3, down] + r3[n, 1, one].astype(F32)).astype(BF16)
         c = send_all(s4, r4, last, 3)
         yield
         arrive(c)
-        return [own[n, 0] + r4[n, 0].astype(F32) + r4[n, 1].astype(F32) for n in range(2)]
+        res = [[None, None] for _ in kinds]
+        for m, (n, acc, q, one, two, up, down) in enumerate(each()):
+            res[m // 2][n] = own[n, 0, two] + r4[n, 0, two].astype(F32) + r4[n, 1, two].astype(F32)
+        return res
 
     def plane_gather(g, slot):
         h, q = TILE // 2, TILE // 4
@@ -225,6 +250,10 @@
         gather = plane_gather(g, slot)
         next(gather)
         if k == 0:
+            places.wait()
+            found = find_slots()
+            found.start()
+            found.wait()
             loads[2].wait()
             tiles[TILE] = jnp.zeros((TILE, TILE), BF16)
             lay_out(3, 3)
@@ -241,7 +270,7 @@
             part[first:last] = value.reshape(last - first, SLAB, hc)
 
         def send_z(step, up, down):
-            return [send(*up, zp, slot + 16 + step % 2), send(*down, zm, slot + 18 + step % 2)]
+            return [send(*up, zp, slot + 8 + step % 2), send(*down, zm, slot + 10 + step % 2)]
 
         top, low = slice(0, HALF), slice(HALF, SLAB)
         slabs(3, 6)
@@ -310,85 +339,59 @@
         out.start()
         outs.append(out)
 
-    def sum_back(k):
+    def plane_sums(k):
         hc = WIDTHS[k]
         cols = slice(FIRST[k], FIRST[k] + hc)
-        bpart, back = r["bpart" + str(k)], r["back" + str(k)]
-
-        def term(i, j, lo, hi):
-            return bpart[i, j, lo:hi].astype(F32)
-
-        res = yield from scatter_sum(term, sum_refs("b", k), TILE // 4, SLOTS * k)
-        back[0 : TILE // 2] = res[0].astype(BF16)
-        back[TILE // 2 : TILE] = res[1].astype(BF16)
-        theirs = f32dot(back[...], weight[pl.ds(pl.multiple_of((1 - f) * WIDE, WIDE), WIDE), cols], DN_N)
-        if k > 0:
-            theirs += terms[1]
-        if k < LAST:
-            terms[1] = theirs
-        else:
-            terms_send[...] = theirs.astype(BF16)
-            swap = [send(terms_send, terms_recv, other, SLOTS * PARTS + 9)]
-        mine = f32dot(back[...], weight[pl.ds(pl.multiple_of(f * WIDE, WIDE), WIDE), cols], DN_N)
-        if k > 0:
-            mine += terms[0]
-        terms[0] = mine
-        if k == LAST:
-            yield
-            arrive(swap)
-            igrad[...] = (terms[0] + terms_recv[...].astype(F32)).astype(BF16)
-
-    def sum_weight(k):
-        hc = WIDTHS[k]
-        cols = slice(FIRST[k], FIRST[k] + hc)
-        bpart, wpart, wown, wz = (r[n + str(k)] for n in ("bpart", "wpart", "wown", "wz"))
+        bpart, wpart = r["bpart" + str(k)], r["wpart" + str(k)]
         block = bpart[...].reshape(ROWS, hc)
         for n in range(2):
             value = f32dot(nodes[n].reshape(ROWS, WIDE), block, DN_T)
             wpart[n * WIDE : (n + 1) * WIDE] = value * ((ROWS * DEPTH) ** -0.5)
 
-        def term(i, j, lo, hi):
+        def bterm(i, j, lo, hi):
+            return bpart[i, j, lo:hi].astype(F32)
+
+        def wterm(i, j, lo, hi):
             start = (((y + i) % SIDE) * SIDE + (x + j) % SIDE) * (INNER // 16) + lo
             return wpart[pl.ds(pl.multiple_of(start, 16), hi - lo)]
 
-        res = yield from scatter_sum(term, sum_refs("w", k), 16, SLOTS * k + 8)
-        wown[0:32] = res[0]
-        wown[32:64] = res[1]
-        slot = SLOTS * k + 20
+        bufs = [r["sum_" + n + str(k)] for n in ("s1", "s2", "s3", "s4", "r1", "r2", "r3", "r4", "own")]
+        res = yield from scatter_sum(((bterm, TILE // 4), (wterm, INNER // 64)), bufs, SLOTS * k)
+        for n in range(2):
+            wown[n * 32 : (n + 1) * 32, cols] = res[1][n]
+            back[n * TILE // 2 : (n + 1) * TILE // 2, cols] = res[0][n].astype(BF16)
+
+    def finish():
+        slot = SLOTS * PARTS + 9
         for d in range(1, DEPTH):
             start = pl.multiple_of(((z + d) % DEPTH) * 8, 8)
             send(wown.at[pl.ds(start, 8)], wz.at[d], zpeer[d], slot)
-        yield
+        theirs = f32dot(back[...], weight[pl.ds(pl.multiple_of((1 - f) * WIDE, WIDE), WIDE)], DN_N)
+        terms_send[...] = theirs.astype(BF16)
+        swap = [send(terms_send, terms_recv, other, slot + 1)]
+        mine = f32dot(back[...], weight[pl.ds(pl.multiple_of(f * WIDE, WIDE), WIDE)], DN_N)
+        total = wown[pl.ds(pl.multiple_of(z * 8, 8), 8)]
+        arrive(swap)
+        igrad[...] = (mine + terms_recv[...].astype(F32)).astype(BF16)
         others = wz.at[1:DEPTH]
         pltpu.make_async_copy(others, others, recv_sem.at[slot]).wait()
         pltpu.make_async_copy(others, others, send_sem.at[slot]).wait()
-        total = wown[pl.ds(pl.multiple_of(z * 8, 8), 8)]
         for d in range(1, DEPTH):
             total = total + wz[d]
-        wgrad[:, cols] = total
-
-    def sum_refs(kind, k):
-        return [r[kind + n + str(k)] for n in ("s1", "s2", "s3", "s4", "r1", "r2", "r3", "r4", "acc")]
+        wgrad[...] = total
+        yield
 
     outs = []
-    flows = [make(k) for make in (flow, sum_back, sum_weight) for k in range(PARTS)] + [gather_features()]
+    flows = [make(k) for make in (flow, plane_sums) for k in range(PARTS)] + [gather_features(), finish()]
     for n in ORDER:
         next(flows[n], None)
     for out in outs:
         out.wait()
 
 
-def slot_table(coords, count):
-    place = coords[:, 0] * (SIDE * SIDE) + coords[:, 1]
-    slot = jnp.arange(TILE, dtype=jnp.int32)
-    cell = jnp.arange(SIDE * SIDE * SIDE * SIDE, dtype=jnp.int32)
-    hit = (place[None, :] == cell[:, None]) & (slot[None, :] < count)
-    return jnp.min(jnp.where(hit, slot[None, :], TILE), axis=1)
-
-
 def scratch_of():
     dma = pltpu.SemaphoreType.DMA
-    slots = SLOTS * PARTS + 10
+    slots = SLOTS * PARTS + 11
     refs = {
         "tiles": VMEM((TILE + 1, TILE, TILE), BF16),
         "adj": VMEM((ROWS, ROWS), BF16),
@@ -397,11 +400,16 @@
         "gout": VMEM((ROWS, WIDE), BF16),
         "layer": VMEM((ROWS, WIDE), BF16),
         "nodes": VMEM((2, SIDE, SIDE, TILE, WIDE), BF16),
-        "terms": VMEM((2, TILE, WIDE), F32),
+        "back": VMEM((TILE, WIDE), BF16),
+        "wown": VMEM((INNER // 16, WIDE), F32),
+        "wz": VMEM((DEPTH, 8, WIDE), F32),
+        "coords": VMEM((2, TILE), jnp.int32),
+        "table": VMEM((1, SIDE**4), jnp.int32),
+        "slot_of": pltpu.SMEM((1, SIDE**4), jnp.int32),
         "terms_send": VMEM((TILE, WIDE), BF16),
         "terms_recv": VMEM((TILE, WIDE), BF16),
-        "local_sem": dma((3 + len(WIDTHS),)),
-        "out_sem": dma((len(WIDTHS),)),
+        "local_sem": dma((5 + PARTS,)),
+        "out_sem": dma((PARTS,)),
         "send_sem": dma((slots,)),
         "recv_sem": dma((slots,)),
     }
@@ -417,18 +425,15 @@
             "delta": ((ROWS, hc), BF16),
             "bsum": ((ROWS, hc), F32),
             "bpart": ((SIDE, SIDE, TILE, hc), BF16),
-            "back": ((TILE, hc), BF16),
             "wpart": ((INNER, hc), F32),
-            "wown": ((INNER // 16, hc), F32),
-            "wz": ((DEPTH, 8, hc), F32),
         }
-        for kind, q in (("b", TILE // 4), ("w", INNER // 64)):
-            for way in "sr":
-                shapes[kind + way + "1"] = ((2, 2, SIDE, q, hc), BF16)
-                shapes[kind + way + "2"] = ((2, 2, SIDE, 2 * q, hc), BF16)
-                shapes[kind + way + "3"] = ((2, 2, q, hc), BF16)
-                shapes[kind + way + "4"] = ((2, 2, 2 * q, hc), BF16)
-            shapes[kind + "acc"] = ((2, SIDE, 2 * q, hc), F32)
+        q = TILE // 4 + INNER // 64
+        for way in "sr":
+            shapes["sum_" + way + "1"] = ((2, 2, SIDE, q, hc), BF16)
+            shapes["sum_" + way + "2"] = ((2, 2, SIDE, 2 * q, hc), BF16)
+            shapes["sum_" + way + "3"] = ((2, 2, q, hc), BF16)
+            shapes["sum_" + way + "4"] = ((2, 2, 2 * q, hc), BF16)
+        shapes["sum_own"] = ((2, SIDE, 2 * q, hc), F32)
         for name, (shape, dtype) in shapes.items():
             refs[name + str(k)] = VMEM(shape, dtype)
     return refs
@@ -436,7 +441,7 @@
 
 def on_device(tiles, coords, counts, features, weight, grad_out):
     scratch = scratch_of()
-    anywhere = pl.BlockSpec(memory_space=pl.ANY)
+    anywhere, hbm = pl.BlockSpec(memory_space=pl.ANY), pl.BlockSpec(memory_space=pltpu.HBM)
     shapes = (
         jax.ShapeDtypeStruct((ROWS, WIDE), BF16),
         jax.ShapeDtypeStruct((8, WIDE), F32),
@@ -445,7 +450,7 @@
     return pl.pallas_call(
         functools.partial(kernel, tuple(scratch)),
         out_shape=shapes,
-        in_specs=[pl.BlockSpec(memory_space=pltpu.SMEM)] + [anywhere] * 4,
+        in_specs=[pl.BlockSpec(memory_space=pltpu.SMEM)] + [hbm] * 5,
         out_specs=(anywhere, pl.BlockSpec(memory_space=VMEM), pl.BlockSpec(memory_space=VMEM)),
         scratch_shapes=list(scratch.values()),
         compiler_params=pltpu.CompilerParams(
@@ -453,7 +458,7 @@
         ),
         cost_estimate=pl.CostEstimate(flops=11 * 10**9, bytes_accessed=10 * 2**20, transcendentals=2**20),
         name="graph_layer",
-    )(slot_table(coords[0, 0], counts[0, 0]), tiles[0, 0], features, weight, grad_out)
+    )(counts, coords[0, 0].T, tiles[0, 0], features, weight, grad_out)
 
 def solution(mesh):
     return jax.shard_map(

time: 112 us -> 108 us (0.964)
  Pallas kernels: 104 us -> 101 us
  other arithmetic: 1.45 us -> 0 us
    pallas_call x1, Pallas kernels: 104 us -> 101 us  [on_device(): pl.pallas_call(functools.partial(kernel, tuple(scratch)), out_shape=shape...]
    unnamed x7 -> x9, local copies, waits for them, and re-layouts: 4.35 us -> 5.43 us
where the time goes in v4:
time: 108 us
  Pallas kernels  101 us (94%)
  local copies, waits for them, and re-layouts  5.43 us (5%)
  between operations  1.3 us (1%)
    pallas_call x1, Pallas kernels, on_device(): pl.pallas_call(functools.partial(kernel, tuple(scratch)), out_shape=shape...  101 us
    unnamed x9, local copies, waits for them, and re-layouts  5.43 us

profile of v4, /device:TPU:2, one launch (start us, length us, event | category | flops | bytes accessed | tf_op | source)
XLA Modules:
  0.0 107.7 jit_solution(16686087268055321188)
XLA Ops:
  1.3 0.0 copy-start
  1.3 1.2 %copy-done = bf16[1024,512]{1,0:T(8,128)(2,1)S(1)} copy-done((bf16[1024,512]{1,0:T(8,128)(2,1)S(1)}, bf16[1024,512]{1,0:T(8,128)(2,1)}, u32[]{:S(2)}) %copy-start) | copy-done | bytes 1048600
  2.5 0.0 copy-start.1
  2.5 0.9 copy-done.1
  3.5 0.0 copy-start.2
  3.5 0.7 copy-done.2
  4.1 100.9 %graph_layer.1 = (bf16[2048,512]{1,0:T(8,128)(2,1)S(1)}, f32[8,512]{1,0:T(8,128)S(1)}, bf16[128,512]{1,0:T(8,128)(2,1)S(1)}) custom-call(s32[1,1]{1,0:T(1,128)S(6)} %copy.12.counts, s32[2,128]{1,0:T(2,128)S(1)} %bitcast.4, bf16[128,128,128]{2,1,0:T(8,128)(2,1)} %bitcast.5, bf16[128,1024]{1,0:T(8,128)(2,1)S(1)} %copy-done.1, bf16[1024,512]{1,0:T(8,128)(2,1)S(1)} %copy-done, ...), custom_call_target="tpu_custom_call" | custom-call | flops 11000000512 | bytes 10485760 | tf_op jit(solution)/shard_map/graph_layer/pallas_call | solution.py:450
  105.1 1.3 %copy.13 = bf16[2048,512]{1,0:T(8,128)(2,1)} copy(bf16[2048,512]{1,0:T(8,128)(2,1)S(1)} %get-tuple-element.6) | data formatting | bytes 4194304
  106.4 0.6 copy.14
  107.0 0.7 copy.15
Async XLA Ops:
  1.3 1.2 %copy-start = (bf16[1024,512]{1,0:T(8,128)(2,1)S(1)}, bf16[1024,512]{1,0:T(8,128)(2,1)}, u32[]{:S(2)}) copy-start(bf16[1024,512]{1,0:T(8,128)(2,1)} %weight_hbm.1) | copy-start | bytes 3145732
  2.5 0.9 copy-start.1
  3.5 0.7 copy-start.2

commit v5 on v4

--- a/solution.py
+++ b/solution.py
@@ -23,12 +23,15 @@
 INNER = 1024
 WIDTHS = (256, 256)
 PARTS = len(WIDTHS)
+CUTS = (1, 2)
 ORDER = (
-    0, 1, 0, 1, 0, 1, 0, 4, 1, 0, 1, 0, 1, 4, 0, 4, 1, 0, 1, 0, 1, 4, 0, 4, 1, 0, 1, 0, 1, 4,
-    0, 2, 1, 3, 2, 3, 2, 3, 2, 3, 2, 3, 5,
+    0, 1, 0, 1, 0, 1, 0, 5, 1, 0, 1, 5, 0, 1, 5, 0, 1, 0, 5, 1, 0, 1, 0, 1, 5, 0, 1, 0, 1, 5,
+    0, 2, 1, 3, 4, 2, 4, 3, 2, 4, 3, 2, 4, 3, 2, 4, 3, 6,
 )
 FIRST = [sum(WIDTHS[:k]) for k in range(len(WIDTHS))]
 LAST = PARTS - 1
+PIECES = [(k, n) for k in range(PARTS) for n in range(CUTS[k])]
+LATER = [p for p in PIECES if p[1] > 0]
 SLOTS = 12
 
 DN_T = (((0,), (0,)), ((), ()))
@@ -339,24 +342,27 @@
         out.start()
         outs.append(out)
 
-    def plane_sums(k):
+    def plane_sums(k, piece):
         hc = WIDTHS[k]
-        cols = slice(FIRST[k], FIRST[k] + hc)
+        wide = hc // CUTS[k]
+        inner = slice(piece * wide, (piece + 1) * wide)
+        cols = slice(FIRST[k] + inner.start, FIRST[k] + inner.stop)
         bpart, wpart = r["bpart" + str(k)], r["wpart" + str(k)]
-        block = bpart[...].reshape(ROWS, hc)
-        for n in range(2):
-            value = f32dot(nodes[n].reshape(ROWS, WIDE), block, DN_T)
-            wpart[n * WIDE : (n + 1) * WIDE] = value * ((ROWS * DEPTH) ** -0.5)
+        if piece == 0:
+            block = bpart[...].reshape(ROWS, hc)
+            for n in range(2):
+                value = f32dot(nodes[n].reshape(ROWS, WIDE), block, DN_T)
+                wpart[n * WIDE : (n + 1) * WIDE] = value * ((ROWS * DEPTH) ** -0.5)
 
         def bterm(i, j, lo, hi):
-            return bpart[i, j, lo:hi].astype(F32)
+            return bpart[i, j, lo:hi, inner].astype(F32)
 
         def wterm(i, j, lo, hi):
             start = (((y + i) % SIDE) * SIDE + (x + j) % SIDE) * (INNER // 16) + lo
-            return wpart[pl.ds(pl.multiple_of(start, 16), hi - lo)]
-
-        bufs = [r["sum_" + n + str(k)] for n in ("s1", "s2", "s3", "s4", "r1", "r2", "r3", "r4", "own")]
-        res = yield from scatter_sum(((bterm, TILE // 4), (wterm, INNER // 64)), bufs, SLOTS * k)
+            return wpart[pl.ds(pl.multiple_of(start, 16), hi - lo), inner]
+
+        bufs = [r["sum_" + n + str(k) + str(piece)] for n in ("s1", "s2", "s3", "s4", "r1", "r2", "r3", "r4", "own")]
+        res = yield from scatter_sum(((bterm, TILE // 4), (wterm, INNER // 64)), bufs, SLOTS * k if piece == 0 else SLOTS * PARTS + 11 + 8 * LATER.index((k, piece)))
         for n in range(2):
             wown[n * 32 : (n + 1) * 32, cols] = res[1][n]
             back[n * TILE // 2 : (n + 1) * TILE // 2, cols] = res[0][n].astype(BF16)
@@ -382,7 +388,7 @@
         yield
 
     outs = []
-    flows = [make(k) for make in (flow, plane_sums) for k in range(PARTS)] + [gather_features(), finish()]
+    flows = [flow(k) for k in range(PARTS)] + [plane_sums(k, n) for k, n in PIECES] + [gather_features(), finish()]
     for n in ORDER:
         next(flows[n], None)
     for out in outs:
@@ -391,7 +397,7 @@
 
 def scratch_of():
     dma = pltpu.SemaphoreType.DMA
-    slots = SLOTS * PARTS + 11
+    slots = SLOTS * PARTS + 11 + 8 * len(LATER)
     refs = {
         "tiles": VMEM((TILE + 1, TILE, TILE), BF16),
         "adj": VMEM((ROWS, ROWS), BF16),
@@ -427,15 +433,16 @@
             "bpart": ((SIDE, SIDE, TILE, hc), BF16),
             "wpart": ((INNER, hc), F32),
         }
-        q = TILE // 4 + INNER // 64
-        for way in "sr":
-            shapes["sum_" + way + "1"] = ((2, 2, SIDE, q, hc), BF16)
-            shapes["sum_" + way + "2"] = ((2, 2, SIDE, 2 * q, hc), BF16)
-            shapes["sum_" + way + "3"] = ((2, 2, q, hc), BF16)
-            shapes["sum_" + way + "4"] = ((2, 2, 2 * q, hc), BF16)
-        shapes["sum_own"] = ((2, SIDE, 2 * q, hc), F32)
+        q, wide = TILE // 4 + INNER // 64, hc // CUTS[k]
+        for piece in range(CUTS[k]):
+            for way in "sr":
+                shapes[f"sum_{way}1{k}{piece}"] = ((2, 2, SIDE, q, wide), BF16)
+                shapes[f"sum_{way}2{k}{piece}"] = ((2, 2, SIDE, 2 * q, wide), BF16)
+                shapes[f"sum_{way}3{k}{piece}"] = ((2, 2, q, wide), BF16)
+                shapes[f"sum_{way}4{k}{piece}"] = ((2, 2, 2 * q, wide), BF16)
+            shapes[f"sum_own{k}{piece}"] = ((2, SIDE, 2 * q, wide), F32)
         for name, (shape, dtype) in shapes.items():
-            refs[name + str(k)] = VMEM(shape, dtype)
+            refs[name if name.startswith("sum_") else name + str(k)] = VMEM(shape, dtype)
     return refs
 
 
@@ -447,6 +454,7 @@
         jax.ShapeDtypeStruct((8, WIDE), F32),
         jax.ShapeDtypeStruct((TILE, WIDE), BF16),
     )
+    large = (coords[0, 0].T, tiles[0, 0], features, weight, grad_out)
     return pl.pallas_call(
         functools.partial(kernel, tuple(scratch)),
         out_shape=shapes,
@@ -458,7 +466,7 @@
         ),
         cost_estimate=pl.CostEstimate(flops=11 * 10**9, bytes_accessed=10 * 2**20, transcendentals=2**20),
         name="graph_layer",
-    )(counts, coords[0, 0].T, tiles[0, 0], features, weight, grad_out)
+    )(counts, *[pltpu.with_memory_space_constraint(v, pltpu.HBM) for v in large])
 
 def solution(mesh):
     return jax.shard_map(

time: 108 us -> 105 us (0.972)
  local copies, waits for them, and re-layouts: 5.43 us -> 2.58 us
    unnamed x9 -> x3, local copies, waits for them, and re-layouts: 5.43 us -> 2.58 us
where the time goes in v5:
time: 105 us; the launch traced here: 104 us
  Pallas kernels  100 us (95%)
  local copies, waits for them, and re-layouts  2.58 us (2%)
  between operations  1.29 us (1%)
    pallas_call x1, Pallas kernels, on_device(): pl.pallas_call(functools.partial(kernel, tuple(scratch)), out_shape=shape...  100 us
    unnamed x3, local copies, waits for them, and re-layouts  2.58 us

profile of v5, /device:TPU:2, one launch (start us, length us, event | category | flops | bytes accessed | tf_op | source)
XLA Modules:
  0.0 104.2 jit_solution(12254770008447399752)
XLA Ops:
  1.3 100.3 %graph_layer.1 = (bf16[2048,512]{1,0:T(8,128)(2,1)S(1)}, f32[8,512]{1,0:T(8,128)S(1)}, bf16[128,512]{1,0:T(8,128)(2,1)S(1)}) custom-call(s32[1,1]{1,0:T(1,128)S(6)} %copy.12.counts, s32[2,128]{1,0:T(2,128)} %bitcast.5, bf16[128,128,128]{2,1,0:T(8,128)(2,1)} %bitcast.4, bf16[128,1024]{1,0:T(8,128)(2,1)} %feat_hbm.1, bf16[1024,512]{1,0:T(8,128)(2,1)} %weight_hbm.1, ...), custom_call_target="tpu_custom_call" | custom-call | flops 11000000512 | bytes 10485760 | tf_op jit(solution)/shard_map/graph_layer/pallas_call | solution.py:458
  101.6 1.3 %copy.13 = bf16[2048,512]{1,0:T(8,128)(2,1)} copy(bf16[2048,512]{1,0:T(8,128)(2,1)S(1)} %get-tuple-element.6) | data formatting | bytes 4194304
  102.9 0.6 copy.14
  103.5 0.7 copy.15

commit v6 on v5

--- a/solution.py
+++ b/solution.py
@@ -32,7 +32,7 @@
 LAST = PARTS - 1
 PIECES = [(k, n) for k in range(PARTS) for n in range(CUTS[k])]
 LATER = [p for p in PIECES if p[1] > 0]
-SLOTS = 12
+SLOTS = 4
 
 DN_T = (((0,), (0,)), ((), ()))
 DN_N = (((1,), (1,)), ((), ()))
@@ -94,11 +94,10 @@
         copy.start()
         return copy
 
-    def arrive(copies):
-        for copy in copies:
-            copy.wait_recv()
-        for copy in copies:
-            copy.wait_send()
+    def arrive(flight):
+        whole, slot = flight
+        pltpu.make_async_copy(whole, whole, recv_sem.at[slot]).wait()
+        pltpu.make_async_copy(whole, whole, send_sem.at[slot]).wait()
 
     def find_slots():
         shape = (SIDE**4, TILE)
@@ -129,11 +128,10 @@
         first, last = ((2, 3), (0, 1)), ((0, 1), (2, 3))
 
         def send_all(src, dst, to, phase):
-            return [
-                send(src.at[n, d], dst.at[n, d], ways[to[n][d]], slot + 2 * to[n][d] + phase % 2)
-                for n in range(2)
-                for d in range(2)
-            ]
+            for n in range(2):
+                for d in range(2):
+                    send(src.at[n, d], dst.at[n, d], ways[to[n][d]], slot + phase % 2)
+            return src, slot + phase % 2
 
         def each():
             at_q = 0
@@ -194,10 +192,10 @@
         h, q = TILE // 2, TILE // 4
 
         def send_all(phase, *moves):
-            return [
-                send(src, dst, to, slot + 2 * n + phase % 2)
-                for n, (src, dst, to) in enumerate(zip(moves[0::2], moves[1::2], (xp, xm, yp, ym)))
-            ]
+            for src, dst, to in zip(moves[0::2], moves[1::2], (xp, xm, yp, ym)):
+                send(src, dst, to, slot + phase % 2)
+            whole = (g.at[0, 0:2], g.at[0, 0], g.at[0:2], g.at[0])[phase]
+            return whole, slot + phase % 2
 
         own_h, own_l = g.at[0, 0, 0:h], g.at[0, 0, h:TILE]
         c = send_all(
@@ -234,7 +232,8 @@
                 nodes[n, 0, 0] = feat[:, n * WIDE : (n + 1) * WIDE]
 
         yield from plane_gather(mine, SLOTS * PARTS)
-        c = [send(mine, nodes.at[f], other, SLOTS * PARTS + 8)]
+        send(mine, nodes.at[f], other, SLOTS * PARTS + 2)
+        c = mine, SLOTS * PARTS + 2
         yield
         arrive(c)
 
@@ -273,7 +272,9 @@
             part[first:last] = value.reshape(last - first, SLAB, hc)
 
         def send_z(step, up, down):
-            return [send(*up, zp, slot + 8 + step % 2), send(*down, zm, slot + 10 + step % 2)]
+            send(*up, zp, slot + 2 + step % 2)
+            send(*down, zm, slot + 2 + step % 2)
+            return (pre.at[0] if step in (3, 7) else pre.at[0:2]), slot + 2 + step % 2
 
         top, low = slice(0, HALF), slice(HALF, SLAB)
         slabs(3, 6)
@@ -362,26 +363,24 @@
             return wpart[pl.ds(pl.multiple_of(start, 16), hi - lo), inner]
 
         bufs = [r["sum_" + n + str(k) + str(piece)] for n in ("s1", "s2", "s3", "s4", "r1", "r2", "r3", "r4", "own")]
-        res = yield from scatter_sum(((bterm, TILE // 4), (wterm, INNER // 64)), bufs, SLOTS * k if piece == 0 else SLOTS * PARTS + 11 + 8 * LATER.index((k, piece)))
+        res = yield from scatter_sum(((bterm, TILE // 4), (wterm, INNER // 64)), bufs, SLOTS * k if piece == 0 else SLOTS * PARTS + 5 + 2 * LATER.index((k, piece)))
         for n in range(2):
             wown[n * 32 : (n + 1) * 32, cols] = res[1][n]
             back[n * TILE // 2 : (n + 1) * TILE // 2, cols] = res[0][n].astype(BF16)
 
     def finish():
-        slot = SLOTS * PARTS + 9
+        slot = SLOTS * PARTS + 3
         for d in range(1, DEPTH):
             start = pl.multiple_of(((z + d) % DEPTH) * 8, 8)
             send(wown.at[pl.ds(start, 8)], wz.at[d], zpeer[d], slot)
         theirs = f32dot(back[...], weight[pl.ds(pl.multiple_of((1 - f) * WIDE, WIDE), WIDE)], DN_N)
         terms_send[...] = theirs.astype(BF16)
-        swap = [send(terms_send, terms_recv, other, slot + 1)]
+        send(terms_send, terms_recv, other, slot + 1)
         mine = f32dot(back[...], weight[pl.ds(pl.multiple_of(f * WIDE, WIDE), WIDE)], DN_N)
         total = wown[pl.ds(pl.multiple_of(z * 8, 8), 8)]
-        arrive(swap)
+        arrive((terms_send, slot + 1))
         igrad[...] = (mine + terms_recv[...].astype(F32)).astype(BF16)
-        others = wz.at[1:DEPTH]
-        pltpu.make_async_copy(others, others, recv_sem.at[slot]).wait()
-        pltpu.make_async_copy(others, others, send_sem.at[slot]).wait()
+        arrive((wz.at[1:DEPTH], slot))
         for d in range(1, DEPTH):
             total = total + wz[d]
         wgrad[...] = total
@@ -397,7 +396,7 @@
 
 def scratch_of():
     dma = pltpu.SemaphoreType.DMA
-    slots = SLOTS * PARTS + 11 + 8 * len(LATER)
+    slots = SLOTS * PARTS + 5 + 2 * len(LATER)
     refs = {
         "tiles": VMEM((TILE + 1, TILE, TILE), BF16),
         "adj": VMEM((ROWS, ROWS), BF16),

time: 105 us -> 104 us (level)
  no operation moved by 1% of the time
where the time goes in v6:
time: 104 us
  Pallas kernels  99.8 us (96%)
  local copies, waits for them, and re-layouts  2.58 us (2%)
  between operations  1.29 us (1%)
    pallas_call x1, Pallas kernels, on_device(): pl.pallas_call(functools.partial(kernel, tuple(scratch)), out_shape=shape...  99.8 us
    unnamed x3, local copies, waits for them, and re-layouts  2.58 us

profile of v6, /device:TPU:2, one launch (start us, length us, event | category | flops | bytes accessed | tf_op | source)
XLA Modules:
  0.0 103.6 jit_solution(7989607431763531029)
XLA Ops:
  1.3 99.8 %graph_layer.1 = (bf16[2048,512]{1,0:T(8,128)(2,1)S(1)}, f32[8,512]{1,0:T(8,128)S(1)}, bf16[128,512]{1,0:T(8,128)(2,1)S(1)}) custom-call(s32[1,1]{1,0:T(1,128)S(6)} %copy.12.counts, s32[2,128]{1,0:T(2,128)} %bitcast.5, bf16[128,128,128]{2,1,0:T(8,128)(2,1)} %bitcast.4, bf16[128,1024]{1,0:T(8,128)(2,1)} %feat_hbm.1, bf16[1024,512]{1,0:T(8,128)(2,1)} %weight_hbm.1, ...), custom_call_target="tpu_custom_call" | custom-call | flops 11000000512 | bytes 10485760 | tf_op jit(solution)/shard_map/graph_layer/pallas_call | solution.py:457
  101.1 1.3 %copy.13 = bf16[2048,512]{1,0:T(8,128)(2,1)} copy(bf16[2048,512]{1,0:T(8,128)(2,1)S(1)} %get-tuple-element.6) | data formatting | bytes 4194304
  102.4 0.6 copy.14
  103.0 0.7 copy.15
